TPU v7x, 128 devices: a whole 4x4x4 slice. The times are simulated.
128 devices in a mesh: seq: 16 (over y_lo, z, core), exp: 8 (over y_hi, x).
Axes of the slice: x: 4, y: 4 (y_hi: 2, y_lo: 2; y = y_hi * 2 + y_lo), z: 4, core: 2. Of those that a mesh axis runs over, the one named last changes fastest.
Arguments:
- queries: bfloat16 [8, 2048, 8192], P('exp', 'seq'), may hold values from -70 to 70
- key_vectors_rows: bfloat16 [8, 2048, 512], P('exp', 'seq'), may hold values from -70 to 70
- values: bfloat16 [8, 2048, 512], P('exp', 'seq'), may hold values from -6 to 6
- expert_tokens: bfloat16 [16384, 4096], P(('seq', 'exp')), may hold values from -6 to 6
- routed_experts: int32 [16384, 8], P(('seq', 'exp')), may hold values from 0 to 127, all different within a row; in each aligned block of 128 rows (0 to 127, 128 to 255, ...) at most 9 rows name the same one
- gate_weights: float32 [16384, 8], P(('seq', 'exp')), may hold values from 0.05 to 0.25
- gate_up_weight: bfloat16 [128, 4096, 1536], P(('seq', 'exp')), may hold values from -0.09375 to 0.09375
- down_weight: bfloat16 [128, 768, 4096], P(('seq', 'exp')), may hold values from -0.21875 to 0.21875
Outputs:
- attention_out: bfloat16 [8, 2048, 8192], P('exp', 'seq')
- expert_out: bfloat16 [16384, 4096], P(('seq', 'exp'))
Inputs may be any that keep to these rules, and one draw needn't show every extreme that they name: `routed_experts`: in each aligned block of 128 rows (the rows of one device) no expert is named by more than 9 entries, a bound that some block reaches; a row names 8 different experts.
All inputs are finite; a program needn't handle non-finite values.
Results may differ from a plain program's by a relative error of at most 0.011.
Values may be sent and summed in bfloat16 or wider, within the bound.
No kernel may reach another device: no remote copies, remote signals or barrier semaphores. Data moves between devices by JAX's collectives and lax.ppermute only.
A program may use at most 256 MiB of HBM per device.

v0:
```python
import jax
import jax.numpy as jnp
from jax import lax
from jax.sharding import PartitionSpec as P

HEAD_SIZE = 128


def attend(query_group, key_head, value_head, block_size):
    length = query_group.shape[0]
    scale = query_group.shape[2] ** (-0.5)
    pieces = []
    for block_index in range(length // block_size):
        finish = (block_index + 1) * block_size
        query_block = query_group[block_index * block_size : finish]
        scores = (
            jnp.einsum(
                "qhd,kd->hqk", query_block, key_head[:finish], preferred_element_type=jnp.float32
            )
            * scale
        )
        query_pos = block_index * block_size + jnp.arange(block_size, dtype=jnp.int32)
        key_pos = jnp.arange(finish, dtype=jnp.int32)
        scores = jnp.where(key_pos[None, None, :] <= query_pos[None, :, None], scores, -jnp.inf)
        maximum = jnp.max(scores, axis=-1, keepdims=True)
        numerators = jnp.exp(scores - maximum)
        totals = jnp.sum(numerators, axis=-1, keepdims=True)
        weights = (numerators / totals).astype(jnp.bfloat16)
        mixed_rows = jnp.einsum(
            "hqk,kd->qhd", weights, value_head[:finish], preferred_element_type=jnp.float32
        )
        pieces.append(mixed_rows.astype(jnp.bfloat16))
    return jnp.concatenate(pieces, axis=0)


def on_device(
    queries,
    key_vectors_rows,
    values,
    expert_tokens,
    routed_experts,
    gate_weights,
    gate_up_weight,
    down_weight,
):
    seq_count = lax.axis_size("seq")
    row_count = queries.shape[1]
    head_total = queries.shape[2] // HEAD_SIZE
    kv_heads = key_vectors_rows.shape[2] // HEAD_SIZE
    local_heads = head_total // seq_count
    query_split = queries.reshape(row_count, seq_count, local_heads * HEAD_SIZE)
    query_local = lax.all_to_all(query_split, "seq", split_axis=1, concat_axis=0, tiled=True)
    key_whole, value_whole = (
        lax.all_gather(key_vectors_rows, "seq", axis=1, tiled=True),
        lax.all_gather(values, "seq", axis=1, tiled=True),
    )
    kv_index = lax.axis_index("seq") * local_heads // (head_total // kv_heads)
    key_head = lax.dynamic_slice_in_dim(key_whole[0], kv_index * HEAD_SIZE, HEAD_SIZE, 1)
    value_head = lax.dynamic_slice_in_dim(value_whole[0], kv_index * HEAD_SIZE, HEAD_SIZE, 1)
    length = query_local.shape[0]
    block_size = min(length, max(512, length // 8))
    attended = attend(
        query_local.reshape(length, local_heads, HEAD_SIZE), key_head, value_head, block_size
    )
    returned = lax.all_to_all(
        attended.reshape(length, local_heads * HEAD_SIZE),
        "seq",
        split_axis=0,
        concat_axis=1,
        tiled=True,
    )
    attention_out = returned.reshape(1, row_count, head_total * HEAD_SIZE)
    token_rows = expert_tokens.shape[0]
    model_width = expert_tokens.shape[1]
    top_count = routed_experts.shape[1]
    exp_count = lax.axis_size("exp")
    expert_count = seq_count * exp_count
    capacity = 9 * token_rows * top_count // (8 * expert_count)
    flat_ids = routed_experts.reshape(-1)
    onehot = (flat_ids[:, None] == jnp.arange(expert_count, dtype=jnp.int32)[None, :]).astype(
        jnp.int32
    )
    slot_index = jnp.sum(onehot * jnp.cumsum(onehot, axis=0), axis=1) - 1
    places = flat_ids * capacity + slot_index
    source_rows = jnp.arange(token_rows * top_count, dtype=jnp.int32) // top_count
    outgoing = (
        jnp.zeros((expert_count * capacity, model_width), jnp.bfloat16)
        .at[places]
        .set(expert_tokens[source_rows])
    )
    hidden_units = down_weight.shape[1]
    arrived = lax.all_to_all(
        outgoing.reshape(expert_count, capacity, model_width),
        ("seq", "exp"),
        split_axis=0,
        concat_axis=0,
        tiled=True,
    )
    flat_rows = arrived.reshape(-1, model_width)
    projected = jnp.dot(flat_rows, gate_up_weight[0], preferred_element_type=jnp.float32)
    hidden = (jax.nn.silu(projected[:, :hidden_units]) * projected[:, hidden_units:]).astype(
        jnp.bfloat16
    )
    produced = jnp.dot(hidden, down_weight[0], preferred_element_type=jnp.float32).astype(
        jnp.bfloat16
    )
    returned_rows = lax.all_to_all(
        produced.reshape(arrived.shape), ("seq", "exp"), split_axis=0, concat_axis=0, tiled=True
    )
    back_rows = returned_rows.reshape(expert_count * capacity, model_width)
    picked = back_rows[places].astype(jnp.float32) * gate_weights.reshape(-1)[:, None]
    expert_out = jnp.sum(picked.reshape(token_rows, top_count, model_width), axis=1).astype(
        jnp.bfloat16
    )
    return (attention_out, expert_out)


def solution(mesh):
    in_specs = (
        P("exp", "seq", None),
        P("exp", "seq", None),
        P("exp", "seq", None),
        P(("seq", "exp"), None),
        P(("seq", "exp"), None),
        P(("seq", "exp"), None),
        P(("seq", "exp"), None, None),
        P(("seq", "exp"), None, None),
    )
    out_specs = (P("exp", "seq", None), P(("seq", "exp"), None))
    return jax.shard_map(
        on_device, mesh=mesh, in_specs=in_specs, out_specs=out_specs, check_vma=False
    )
```

profile of v0, /device:TPU:39, one launch (start us, length us, event | category | flops | bytes accessed | tf_op | source)
XLA Modules:
  0.0 745.0 jit_solution(16407402675065615121)
XLA Ops:
  7.2 0.0 copy-start
  7.2 0.0 all-gather.5.cloned.1.call-start
  7.2 0.7 all-gather.5.cloned.1.call-update
  7.9 2.4 copy.56
  10.4 2.5 copy.35
  12.8 6.8 all-to-all-start
  19.6 0.2 all-gather.3.cloned.1.call-start
  19.8 0.7 copy.34
  20.6 0.0 all-gather.3.cloned.1.call-update
  20.6 0.1 copy.46
  20.7 0.1 eq.29
  20.8 0.1 eq.25
  20.9 0.1 copy.48
  21.0 0.2 fusion.58
  21.2 0.0 copy-start.2
  21.2 0.8 copy-done.2
  22.1 1.1 broadcast_add_fusion
  23.1 0.1 copy.49
  23.3 0.4 fusion.45
  23.7 0.1 copy.45
  23.8 0.1 mul.94
  23.9 7.7 %gather_fusion = bf16[1024,4096]{1,0:T(8,128)(2,1)} fusion(bf16[128,4096]{1,0:T(8,128)(2,1)S(1)} %copy-done, s32[1024]{0:T(1024)S(1)} %broadcast_clamp_fusion.1), kind=kCustom, calls=%fused_computation | custom fusion | bytes 16781312 | tf_op jit(solution)/shard_map/gather | solution.py:89
  31.6 18.4 %scatter_custom_fusion = bf16[1152,4096]{1,0:T(8,128)(2,1)} fusion(s32[1024]{0:T(1024)S(1)} %bitcast.158, bf16[1024,4096]{1,0:T(8,128)(2,1)} %gather_fusion, bf16[]{:T(256)} %constant.70.clone.1), kind=kCustom, calls=%fused_computation.33 | custom fusion | bytes 9437696 | tf_op jit(solution)/shard_map/scatter | solution.py:89
  50.1 15.1 %reshape.253 = bf16[128,9,4096]{2,1,0:T(8,128)(2,1)} reshape(bf16[1152,4096]{1,0:T(8,128)(2,1)} %scatter_custom_fusion) | data formatting | bytes 18874368 | tf_op jit(solution)/shard_map/reshape | solution.py:93
  65.3 0.1 iota_compare_fusion.3
  65.3 1.2 iota_compare_fusion.2
  66.5 1.5 iota_compare_fusion.1
  68.0 1.8 iota_compare_fusion
  69.8 0.0 all-to-all-done
  69.8 9.7 %all-to-all-start.2 = ((bf16[128,9,4096]{2,1,0:T(8,128)(2,1)}), bf16[128,9,4096]{2,1,0:T(8,128)(2,1)}, u32[]{:S(2)}, u32[]{:S(2)}) async-start(bf16[128,9,4096]{2,1,0:T(8,128)(2,1)} %reshape.253), calls=%async_computation.2 | async-start | bytes 33554432 | tf_op jit(solution)/shard_map/all_to_all | solution.py:92
  79.6 1.2 fusion.100
  80.8 1.2 slice.89
  81.9 0.1 slice.83
  82.1 1.2 slice.77
  83.3 0.1 slice.91
  83.4 0.0 all-gather.5.cloned.1.call-done
  83.4 1.7 fusion.56
  85.1 4.0 fusion.116
  89.1 7.2 fusion.111
  96.3 7.3 fusion.54
  103.6 113.3 %all-gather.3.cloned.1.call-done = bf16[1,2048,512]{1,2,0:T(8,128)(2,1)} async-done(((bf16[1,128,512]{1,2,0:T(8,128)(2,1)}), bf16[1,2048,512]{1,2,0:T(8,128)(2,1)}) %all-gather.3.cloned.1.call-update) | async-done | bytes 2097168 | tf_op jit(solution)/shard_map/all_gather | solution.py:55
  216.9 2.8 fusion.42
  219.7 13.1 %fusion.101 = (f32[4,512]{1,0:T(4,128)S(1)}, f32[4,512,2048]{1,2,0:T(8,128)}) fusion(pred[512,2048]{0,1:T(8,128)(4,1)S(1)} %copy-done.3, bf16[512,4,128]{2,1,0:T(4,128)(2,1)S(1)} %slice.91, bf16[1,2048,512]{2,1,0:T(8,128)(2,1)} %all-gather.5.cloned.1.call-done, s32[]{:T(128)S(6)} %select_n.59), kind=kOutput, calls=%fused_computation.129 | convolution fusion | flops 1090521088 | bytes 18882564 | tf_op jit(solution)/shard_map/sub | solution.py:26
  232.8 4.3 fusion.41
  237.1 13.7 %fusion.110 = (f32[4,512]{1,0:T(4,128)S(1)}, f32[4,512,1536]{1,2,0:T(8,128)}) fusion(f32[1536,512,4]{1,0,2:T(8,128)} %fusion.54, pred[512,1536]{0,1:T(8,128)(4,1)S(1)} %copy-done.4), kind=kOutput, calls=%fused_computation.130 | output fusion | flops 18875904 | bytes 25960448 | tf_op jit(solution)/shard_map/sub | solution.py:26
  250.8 5.7 fusion.40
  256.6 7.2 fusion.39
  263.8 0.3 pad_maximum_fusion
  264.1 0.6 copy.57
  264.7 1.9 copy.44
  266.6 69.3 %all-to-all-done.2 = bf16[128,9,4096]{2,1,0:T(8,128)(2,1)} async-done(((bf16[128,9,4096]{2,1,0:T(8,128)(2,1)}), bf16[128,9,4096]{2,1,0:T(8,128)(2,1)}, u32[]{:S(2)}, u32[]{:S(2)}) %all-to-all-start.2) | async-done | bytes 9437216 | tf_op jit(solution)/shard_map/all_to_all | solution.py:92
  335.9 9.5 %all-to-all-start.1 = ((bf16[16,128,512]{1,2,0:T(8,128)(2,1)}), bf16[16,128,512]{1,2,0:T(8,128)(2,1)S(1)}, u32[]{:S(2)}, u32[]{:S(2)}) async-start(bf16[16,128,512]{1,2,0:T(8,128)(2,1)} %copy.44), calls=%async_computation.1 | async-start | bytes 4194304 | tf_op jit(solution)/shard_map/all_to_all | solution.py:65
  345.4 15.8 %reshape.254 = bf16[1152,4096]{1,0:T(8,128)(2,1)} reshape(bf16[128,9,4096]{2,1,0:T(8,128)(2,1)} %all-to-all-done.2) | data formatting | bytes 18874368 | tf_op jit(solution)/shard_map/reshape | solution.py:99
  361.2 18.2 %fusion.6 = f32[1152,1536]{1,0:T(8,128)S(1)} fusion(bf16[1152,4096]{1,0:T(8,128)(2,1)} %reshape.254, bf16[1,4096,1536]{2,1,0:T(8,128)(2,1)} %param.14), kind=kOutput, calls=%fused_computation.14 | convolution fusion | flops 14495514624 | bytes 29097984 | tf_op jit(solution)/shard_map/dot_general | solution.py:100
  379.5 12.5 %convolution_convert_fusion = bf16[1152,4096]{1,0:T(8,128)(2,1)} fusion(bf16[1,768,4096]{2,1,0:T(8,128)(2,1)} %param.15, f32[1152,1536]{1,0:T(8,128)S(1)} %fusion.6), kind=kOutput, calls=%fused_computation.12 | convolution fusion | flops 7257784320 | bytes 22806528 | tf_op jit(solution)/shard_map/dot_general | solution.py:104
  392.0 15.1 %reshape.255 = bf16[128,9,4096]{2,1,0:T(8,128)(2,1)} reshape(bf16[1152,4096]{1,0:T(8,128)(2,1)} %convolution_convert_fusion) | data formatting | bytes 18874368 | tf_op jit(solution)/shard_map/reshape | solution.py:108
  407.1 0.0 all-to-all-done.1
  407.1 12.7 %all-to-all-start.3 = ((bf16[128,9,4096]{2,1,0:T(8,128)(2,1)}), bf16[128,9,4096]{2,1,0:T(8,128)(2,1)}, u32[]{:S(2)}, u32[]{:S(2)}) async-start(bf16[128,9,4096]{2,1,0:T(8,128)(2,1)} %reshape.255), calls=%async_computation.3 | async-start | bytes 33554432 | tf_op jit(solution)/shard_map/all_to_all | solution.py:107
  419.8 0.1 copy.50
  419.9 2.9 copy.51
  422.8 266.1 %all-to-all-done.3 = bf16[128,9,4096]{2,1,0:T(8,128)(2,1)} async-done(((bf16[128,9,4096]{2,1,0:T(8,128)(2,1)}), bf16[128,9,4096]{2,1,0:T(8,128)(2,1)}, u32[]{:S(2)}, u32[]{:S(2)}) %all-to-all-start.3) | async-done | bytes 9437216 | tf_op jit(solution)/shard_map/all_to_all | solution.py:107
  689.0 15.8 %reshape.256 = bf16[1152,4096]{1,0:T(8,128)(2,1)} reshape(bf16[128,9,4096]{2,1,0:T(8,128)(2,1)} %all-to-all-done.3) | data formatting | bytes 18874368 | tf_op jit(solution)/shard_map/reshape | solution.py:110
  704.8 20.2 %gather_fusion.1 = bf16[1024,4096]{1,0:T(8,128)(2,1)} fusion(bf16[1152,4096]{1,0:T(8,128)(2,1)} %reshape.256, s32[1024]{0:T(1024)S(1)} %broadcast_clamp_fusion), kind=kCustom, calls=%fused_computation.1 | custom fusion | bytes 16781312 | tf_op jit(solution)/shard_map/gather | solution.py:111
  725.0 12.9 %fusion.4 = bf16[128,4096]{1,0:T(8,128)(2,1)} fusion(bf16[1024,4096]{1,0:T(8,128)(2,1)} %gather_fusion.1, f32[128,8]{1,0:T(8,128)S(1)} %copy.50), kind=kLoop, calls=%fused_computation.8 | loop fusion | flops 12058624 | bytes 9441280 | tf_op jit(solution)/shard_map/reduce_sum | solution.py:112
  (31 shorter events, 0.1 us)
Async XLA Ops:
  7.2 16.7 %copy-start = (bf16[128,4096]{1,0:T(8,128)(2,1)S(1)}, bf16[128,4096]{1,0:T(8,128)(2,1)}, u32[]{:S(2)}) copy-start(bf16[128,4096]{1,0:T(8,128)(2,1)} %param.11) | copy-start | bytes 3145732
  7.2 12.6 %copy-start.6 = (bf16[1,128,512]{2,1,0:T(8,128)(2,1)S(1)}, bf16[1,128,512]{2,1,0:T(8,128)(2,1)}, u32[]{:S(2)}) copy-start(bf16[1,128,512]{2,1,0:T(8,128)(2,1)} %param.10) | copy-start | bytes 393220
  7.2 13.4 %copy-start.7 = (s32[128,8]{0,1:T(8,128)S(1)}, s32[128,8]{0,1:T(8,128)}, u32[]{:S(2)}) copy-start(s32[128,8]{0,1:T(8,128)} %param.12) | copy-start | bytes 12292
  7.2 76.2 %all-gather.5.cloned.1.call-start = ((), (), s32[]{:S(2)}) async-start(), calls=%async_computation.5 | async-start | bytes 2228224 | tf_op jit(solution)/shard_map/all_gather | solution.py:54
  12.8 57.0 %all-to-all-start = ((bf16[128,16,512]{2,0,1:T(8,128)(2,1)}), bf16[128,16,512]{2,0,1:T(8,128)(2,1)S(1)}, u32[]{:S(2)}, u32[]{:S(2)}) async-start(bf16[128,16,512]{2,0,1:T(8,128)(2,1)} %copy.35), calls=%async_computation | async-start | bytes 4194304 | tf_op jit(solution)/shard_map/all_to_all | solution.py:52
  19.6 197.3 %all-gather.3.cloned.1.call-start = ((), (), s32[]{:S(2)}) async-start(), calls=%async_computation.4 | async-start | bytes 2228224 | tf_op jit(solution)/shard_map/all_gather | solution.py:55
  21.2 0.8 copy-start.2
  31.6 33.6 %copy-start.8 = (s32[1024,1]{0,1:T(1,128)}, s32[1024,1]{0,1:T(1,128)S(1)}, u32[]{:S(2)}) copy-start(s32[1024,1]{0,1:T(1,128)S(1)} %compare_select_fusion.1) | copy-start | bytes 12292
  69.8 266.1 %all-to-all-start.2 = ((bf16[128,9,4096]{2,1,0:T(8,128)(2,1)}), bf16[128,9,4096]{2,1,0:T(8,128)(2,1)}, u32[]{:S(2)}, u32[]{:S(2)}) async-start(bf16[128,9,4096]{2,1,0:T(8,128)(2,1)} %reshape.253), calls=%async_computation.2 | async-start | bytes 33554432 | tf_op jit(solution)/shard_map/all_to_all | solution.py:92
  83.4 5.7 copy-start.5
  216.9 2.8 copy-start.3
  232.8 4.3 copy-start.4
  335.9 71.2 %all-to-all-start.1 = ((bf16[16,128,512]{1,2,0:T(8,128)(2,1)}), bf16[16,128,512]{1,2,0:T(8,128)(2,1)S(1)}, u32[]{:S(2)}, u32[]{:S(2)}) async-start(bf16[16,128,512]{1,2,0:T(8,128)(2,1)} %copy.44), calls=%async_computation.1 | async-start | bytes 4194304 | tf_op jit(solution)/shard_map/all_to_all | solution.py:65
  407.1 12.7 %copy-start.10 = (f32[128,8]{0,1:T(8,128)S(1)}, f32[128,8]{0,1:T(8,128)}, u32[]{:S(2)}) copy-start(f32[128,8]{0,1:T(8,128)} %param.13) | copy-start | bytes 12292
  407.1 12.8 %copy-start.9 = (s32[1024,1]{0,1:T(1,128)S(1)}, s32[1024,1]{0,1:T(1,128)}, u32[]{:S(2)}) copy-start(s32[1024,1]{0,1:T(1,128)} %copy-done.8) | copy-start | bytes 12292
  407.1 281.9 %all-to-all-start.3 = ((bf16[128,9,4096]{2,1,0:T(8,128)(2,1)}), bf16[128,9,4096]{2,1,0:T(8,128)(2,1)}, u32[]{:S(2)}, u32[]{:S(2)}) async-start(bf16[128,9,4096]{2,1,0:T(8,128)(2,1)} %reshape.255), calls=%async_computation.3 | async-start | bytes 33554432 | tf_op jit(solution)/shard_map/all_to_all | solution.py:107
  704.8 33.1 %copy-start.1 = (bf16[128,4096]{1,0:T(8,128)(2,1)S(1)}, bf16[128,4096]{1,0:T(8,128)(2,1)}, u32[]{:S(2)}) copy-start(bf16[128,4096]{1,0:T(8,128)(2,1)} %param.11) | copy-start | bytes 3145732
Sparse Core Ops, SparseCore 0:
  9.7 52.2 all-gather.4
  63.6 153.2 all-gather.2
where the time goes:
time: 750 us; the launch traced here: 745 us
  waiting for transfers between devices  449 us (60%)
  local copies, waits for them, and re-layouts  125 us (17%)
  matrix products  80 us (11%)
  starting transfers between devices  38.9 us (5%)
  other arithmetic  37.2 us (5%)
  between operations  14.6 us (2%)
    all_to_all x1, waiting for transfers between devices, on_device(): lax.all_to_all(produced.reshape(arrived.shape), ('seq', 'exp'), split_axi...  266 us
    all_gather x1, waiting for transfers between devices, on_device(): lax.all_gather(values, 'seq', axis=1, tiled=True)  113 us
    all_to_all x1, waiting for transfers between devices, on_device(): lax.all_to_all(outgoing.reshape(expert_count, capacity, model_width), ('s...  69.3 us
    sub x2, matrix products, attend(): numerators = jnp.exp(scores - maximum)  20.3 us
    gather x1, local copies, waits for them, and re-layouts, on_device(): back_rows[places].astype(jnp.float32) * gate_weights.reshape(-1)[:, None]  20.2 us
    dot_general x4, matrix products, attend(): jnp.einsum('hqk,kd->qhd', weights, value_head[:finish], preferred_element...  20 us
    scatter x1, local copies, waits for them, and re-layouts, on_device(): outgoing = jnp.zeros((expert_count * capacity, model_width), jnp.bfloat16...  18.4 us
    dot_general x1, matrix products, on_device(): jnp.dot(flat_rows, gate_up_weight[0], preferred_element_type=jnp.float32)  18.2 us
  transfers between devices with their start and end apart: 6, of which 3 were waited for; matrix products, arithmetic and copies ran while one was open for 26% of the time, Pallas kernels for 0%

commit v1 on v0

v1 whole, which is shorter than its diff:
```python
import functools

import jax
import jax.numpy as jnp
from jax import lax
from jax.experimental import pallas as pl
from jax.experimental.pallas import tpu as pltpu
from jax.sharding import PartitionSpec as P

HEAD_SIZE = 128
BAND = 8
FOLD = 512
BF = jnp.bfloat16
F32 = jnp.float32
VMEM = 56 * 1024 * 1024


def iota(shape, dim):
    return lax.broadcasted_iota(jnp.int32, shape, dim)


def dot(a, b):
    return jnp.dot(a, b, preferred_element_type=F32)


def fold_matrix():
    row, col = iota((256, 256), 0), iota((256, 256), 1)
    return (col == (row & 7) * 32 + (row >> 3)).astype(F32).astype(BF)


def unfold_matrix():
    row, col = iota((256, 256), 0), iota((256, 256), 1)
    return (col == (row & 31) * 8 + (row >> 5)).astype(F32).astype(BF)


def ranks(routed):
    tokens = routed.shape[0]
    experts = iota((tokens, 128), 1)
    named = jnp.zeros((tokens, 128), F32)
    for j in range(routed.shape[1]):
        named = jnp.where(routed[:, j : j + 1] == experts, 1.0, named)
    earlier = (iota((tokens, tokens), 1) < iota((tokens, tokens), 0)).astype(F32).astype(BF)
    before = dot(earlier, named.astype(BF))
    return jnp.where(named > 0.5, before, -1.0)


def dispatch_kernel(routed_ref, tokens_ref, out_ref, rank_ref):
    step = pl.program_id(0)
    width = tokens_ref.shape[1]

    @pl.when(step == 0)
    def _():
        rank_ref[...] = ranks(routed_ref[...]).T

    expand = (iota((256, 128), 1) == step * 32 + (iota((256, 128), 0) >> 3)).astype(F32).astype(BF)
    spread = dot(expand, rank_ref[...].astype(BF))
    slot = (iota((256, 128), 0) & 7).astype(F32)
    ninth = rank_ref[pl.ds(pl.multiple_of(step * 32, 32), 32), :]
    pick = jnp.concatenate(
        [jnp.where(spread == slot, 1.0, 0.0), jnp.where(ninth == float(BAND), 1.0, 0.0)], axis=0
    ).astype(BF)
    folded = []
    for c in range(width // FOLD):
        cols = slice(c * FOLD, (c + 1) * FOLD)
        rows = dot(pick, tokens_ref[:, cols]).astype(BF)
        out_ref[:, cols] = rows[:256]
        folded.append(rows[256:])
    out_ref[:, width:] = dot(fold_matrix(), jnp.concatenate(folded, axis=0)).astype(BF)


def dispatch(routed, tokens):
    width = tokens.shape[1]
    return pl.pallas_call(
        dispatch_kernel,
        grid=(4,),
        in_specs=[
            pl.BlockSpec(routed.shape, lambda i: (0, 0)),
            pl.BlockSpec(tokens.shape, lambda i: (0, 0)),
        ],
        out_specs=pl.BlockSpec((256, width + FOLD), lambda i: (i, 0)),
        out_shape=jax.ShapeDtypeStruct((128 * BAND, width + FOLD), BF),
        scratch_shapes=[pltpu.VMEM((128, 128), F32)],
        compiler_params=pltpu.CompilerParams(vmem_limit_bytes=VMEM),
        cost_estimate=pl.CostEstimate(flops=2 * 1152 * 128 * 4096, bytes_accessed=11_000_000, transcendentals=0),
        name="dispatch_rows",
    )(routed, tokens)


def gates_kernel(routed_ref, gates_ref, out_ref):
    routed = routed_ref[...]
    tokens = routed.shape[0]
    rank = ranks(routed)
    experts = iota((tokens, 128), 1)
    gate = jnp.zeros((tokens, 128), F32)
    for j in range(routed.shape[1]):
        gate = jnp.where(routed[:, j : j + 1] == experts, gates_ref[:, j : j + 1], gate)
    high = gate.astype(BF)
    low = (gate - high.astype(F32)).astype(BF)
    wide = 128 * BAND
    expand = (iota((128, wide), 0) == (iota((128, wide), 1) >> 3)).astype(F32).astype(BF)
    chosen = dot(rank.astype(BF), expand) == (iota((tokens, wide), 1) & 7).astype(F32)
    for part, value in enumerate((high, low)):
        rows = slice(part * tokens, (part + 1) * tokens)
        out_ref[rows, :wide] = jnp.where(chosen, dot(value, expand), 0.0).astype(BF)
        out_ref[rows, wide:] = jnp.where(rank == float(BAND), value.astype(F32), 0.0).astype(BF)


def gate_matrix(routed, gates):
    tokens = routed.shape[0]
    return pl.pallas_call(
        gates_kernel,
        out_shape=jax.ShapeDtypeStruct((2 * tokens, 128 * (BAND + 1)), BF),
        compiler_params=pltpu.CompilerParams(vmem_limit_bytes=VMEM),
        cost_estimate=pl.CostEstimate(flops=6 * 128 * 128 * 1024, bytes_accessed=700_000, transcendentals=0),
        name="gate_matrix",
    )(routed, gates)


def experts_kernel(rows_ref, last_ref, up_ref, down_ref, out_ref, ninth_ref, sum_ref, hidden_ref, tail_ref, *, depth_steps):
    step = pl.program_id(0)
    depth = rows_ref.shape[1]
    units = down_ref.shape[0]

    @pl.when(step == 0)
    def _():
        unfold = unfold_matrix()
        for b in range(4):
            piece = dot(unfold, last_ref[b * 256 : (b + 1) * 256, :]).astype(BF)
            for r in range(8):
                at = r * FOLD
                ninth_ref[at // depth, b * 32 : (b + 1) * 32, at % depth : at % depth + FOLD] = piece[
                    r * 32 : (r + 1) * 32
                ]

    @pl.when(step < depth_steps)
    def _():
        rows = jnp.concatenate([rows_ref[...], ninth_ref[step]], axis=0)
        part = dot(rows, up_ref[...])

        @pl.when(step == 0)
        def _():
            sum_ref[...] = part

        @pl.when(step > 0)
        def _():
            sum_ref[...] += part

    @pl.when(step == depth_steps)
    def _():
        gate = sum_ref[:, :units]
        hidden_ref[...] = (gate / (1.0 + jnp.exp(-gate)) * sum_ref[:, units:]).astype(BF)

    @pl.when((step >= depth_steps) & (step < depth_steps + 8))
    def _():
        made = dot(hidden_ref[...], down_ref[...]).astype(BF)
        out_ref[...] = made[:1024]
        tail_ref[step - depth_steps] = made[1024:]

    @pl.when(step == depth_steps + 8)
    def _():
        fold = fold_matrix()
        for b in range(4):
            piece = jnp.concatenate([tail_ref[r, b * 32 : (b + 1) * 32, :] for r in range(8)], axis=0)
            out_ref[b * 256 : (b + 1) * 256, :] = dot(fold, piece).astype(BF)


def run_experts(arrived, up, down, depth=1024):
    rows = arrived.shape[0]
    width = up.shape[1]
    units = down.shape[1]
    depth_steps = width // depth
    all_rows = rows + 128
    return pl.pallas_call(
        functools.partial(experts_kernel, depth_steps=depth_steps),
        grid=(depth_steps + 9,),
        in_specs=[
            pl.BlockSpec((rows, depth), lambda i: (0, jnp.minimum(i, depth_steps - 1))),
            pl.BlockSpec((rows, FOLD), lambda i: (0, width // FOLD)),
            pl.BlockSpec((None, depth, 2 * units), lambda i: (0, jnp.minimum(i, depth_steps - 1), 0)),
            pl.BlockSpec((None, units, FOLD), lambda i: (0, 0, jnp.clip(i - depth_steps, 0, 7))),
        ],
        out_specs=pl.BlockSpec((rows, FOLD), lambda i: (0, jnp.clip(i - depth_steps, 0, 8))),
        out_shape=jax.ShapeDtypeStruct(arrived.shape, BF),
        scratch_shapes=[
            pltpu.VMEM((depth_steps, 128, depth), BF),
            pltpu.VMEM((all_rows, 2 * units), F32),
            pltpu.VMEM((all_rows, units), BF),
            pltpu.VMEM((8, 128, FOLD), BF),
        ],
        compiler_params=pltpu.CompilerParams(vmem_limit_bytes=VMEM),
        cost_estimate=pl.CostEstimate(
            flops=2 * all_rows * units * 3 * width, bytes_accessed=38_000_000, transcendentals=all_rows * units
        ),
        name="run_experts",
    )(arrived, arrived, up, down)


def combine_kernel(gates_ref, rows_ref, last_ref, out_ref, ninth_ref):
    step = pl.program_id(0)
    tokens = out_ref.shape[0]
    wide = rows_ref.shape[0]

    @pl.when(step == 0)
    def _():
        unfold = unfold_matrix()
        for b in range(4):
            piece = dot(unfold, last_ref[b * 256 : (b + 1) * 256, :]).astype(BF)
            for r in range(8):
                ninth_ref[r, b * 32 : (b + 1) * 32, :] = piece[r * 32 : (r + 1) * 32]

    both = dot(gates_ref[:, :wide], rows_ref[...]) + dot(gates_ref[:, wide:], ninth_ref[step])
    out_ref[...] = (both[:tokens] + both[tokens:]).astype(BF)


def combine(gates, returned):
    rows = returned.shape[0]
    width = returned.shape[1] - FOLD
    tokens = gates.shape[0] // 2
    return pl.pallas_call(
        combine_kernel,
        grid=(width // FOLD,),
        in_specs=[
            pl.BlockSpec(gates.shape, lambda i: (0, 0)),
            pl.BlockSpec((rows, FOLD), lambda i: (0, i)),
            pl.BlockSpec((rows, FOLD), lambda i: (0, width // FOLD)),
        ],
        out_specs=pl.BlockSpec((tokens, FOLD), lambda i: (0, i)),
        out_shape=jax.ShapeDtypeStruct((tokens, width), BF),
        scratch_shapes=[pltpu.VMEM((8, 128, FOLD), BF)],
        compiler_params=pltpu.CompilerParams(vmem_limit_bytes=VMEM),
        cost_estimate=pl.CostEstimate(flops=2 * 256 * 1152 * 4096, bytes_accessed=11_000_000, transcendentals=0),
        name="combine_rows",
    )(gates, returned, returned)


def attention_kernel(first_ref, queries_ref, keys_ref, values_ref, out_ref):
    rows = queries_ref.shape[0]
    length = keys_ref.shape[0]
    heads = queries_ref.shape[1] // HEAD_SIZE
    position = first_ref[0] + iota((rows, length), 0)
    seen = iota((rows, length), 1) <= position
    factor = HEAD_SIZE**-0.5 * 1.4426950408889634
    for h in range(heads):
        cols = slice(h * HEAD_SIZE, (h + 1) * HEAD_SIZE)
        scores = lax.dot_general(
            queries_ref[:, cols], keys_ref[...], (((1,), (1,)), ((), ())), preferred_element_type=F32
        )
        scores = jnp.where(seen, scores, -1e30)
        top = jnp.max(scores, axis=-1, keepdims=True)
        part = jnp.exp2((scores - top) * factor)
        total = jnp.sum(part, axis=-1, keepdims=True)
        mixed = dot(part.astype(BF), values_ref[...])
        out_ref[:, cols] = (mixed / total).astype(BF)


def attention(first, queries, pairs, heads_per_step=4):
    rows, width = queries.shape
    length = pairs.shape[0]
    kv_heads = pairs.shape[1] // (2 * HEAD_SIZE)
    steps = width // (heads_per_step * HEAD_SIZE)
    per_kv = steps // kv_heads
    block = (rows, heads_per_step * HEAD_SIZE)
    return pl.pallas_call(
        attention_kernel,
        grid=(steps,),
        in_specs=[
            pl.BlockSpec(memory_space=pltpu.SMEM),
            pl.BlockSpec(block, lambda i: (0, i)),
            pl.BlockSpec((length, HEAD_SIZE), lambda i: (0, i // per_kv)),
            pl.BlockSpec((length, HEAD_SIZE), lambda i: (0, kv_heads + i // per_kv)),
        ],
        out_specs=pl.BlockSpec(block, lambda i: (0, i)),
        out_shape=jax.ShapeDtypeStruct(queries.shape, BF),
        compiler_params=pltpu.CompilerParams(vmem_limit_bytes=VMEM),
        cost_estimate=pl.CostEstimate(
            flops=4 * rows * width * length, bytes_accessed=9_000_000, transcendentals=rows * length * width // HEAD_SIZE
        ),
        name="attention_rows",
    )(first, queries, pairs, pairs)


def on_device(queries, keys, values, tokens, routed, gates, up, down):
    pairs = jnp.concatenate([keys[0], values[0]], axis=1)
    pairs = lax.all_gather(pairs, "seq", axis=0, tiled=True)
    everywhere = ("seq", "exp")
    outgoing = dispatch(routed, tokens)
    arrived = lax.all_to_all(outgoing, everywhere, split_axis=0, concat_axis=0, tiled=True)
    weights = gate_matrix(routed, gates)
    made = run_experts(arrived, up, down)
    made, own = lax.optimization_barrier((made, queries[0]))
    returned = lax.all_to_all(made, everywhere, split_axis=0, concat_axis=0, tiled=True)
    first = (lax.axis_index("seq") * own.shape[0]).astype(jnp.int32).reshape(1)
    attended = attention(first, own, pairs)
    return (attended[None], combine(weights, returned))


def solution(mesh):
    spread = P(("seq", "exp"), None)
    in_specs = (P("exp", "seq", None),) * 3 + (spread,) * 3 + (P(("seq", "exp"), None, None),) * 2
    out_specs = (P("exp", "seq", None), spread)
    return jax.shard_map(on_device, mesh=mesh, in_specs=in_specs, out_specs=out_specs, check_vma=False)
```

time: 750 us -> 378 us (0.50)
  waiting for transfers between devices: 449 us -> 131 us
  local copies, waits for them, and re-layouts: 125 us -> 2.14 us
  blocking collectives: 0 us -> 121 us
  Pallas kernels: 0 us -> 94.4 us
  matrix products: 80 us -> 0 us
  other arithmetic: 37.2 us -> 0.73 us
  starting transfers between devices: 38.9 us -> 7.9 us
    all_to_all x4 -> x1, waiting for transfers between devices: 335 us -> 0.01 us  [on_device(): lax.all_to_all(made, everywhere, split_axis=0, concat_axis=0, tiled=True)]
    all_to_all x0 -> x1, blocking collectives: none -> 121 us  [on_device(): lax.all_to_all(outgoing, everywhere, split_axis=0, concat_axis=0, tiled=T...]
    pallas_call x0 -> x5, Pallas kernels: none -> 94.4 us  [the longest x1 40.3 us: attention(): pl.pallas_call(attention_kernel, grid=(steps,), in_specs=[pl.BlockSpec(me...]
    reshape x5 -> x0, local copies, waits for them, and re-layouts: 64.4 us -> none  [the longest x1 15.8 us: on_device(): flat_rows = arrived.reshape(-1, model_width)]
    dot_general x8 -> x0, matrix products: 59.7 us -> none  [the longest x4 20 us: attend(): jnp.einsum('hqk,kd->qhd', weights, value_head[:finish], preferred_element...]
    all_to_all x4 -> x1, starting transfers between devices: 38.6 us -> 7.67 us  [on_device(): lax.all_to_all(made, everywhere, split_axis=0, concat_axis=0, tiled=True)]
    gather x2 -> x0, local copies, waits for them, and re-layouts: 28 us -> none  [the longest x1 20.2 us: on_device(): back_rows[places].astype(jnp.float32) * gate_weights.reshape(-1)[:, None]]
    sub x2 -> x0, matrix products: 20.3 us -> none  [attend(): numerators = jnp.exp(scores - maximum)]
  transfers between devices with their start and end apart: 6 -> 2, of which waited for: 3 -> 1; matrix products, arithmetic and copies ran while one was open for 26% -> 0% of each run, Pallas kernels for 0% -> 11%
where the time goes in v1:
time: 378 us; the launch traced here: 372 us
  waiting for transfers between devices  131 us (35%)
  blocking collectives  121 us (32%)
  Pallas kernels  94.4 us (25%)
  between operations  14.1 us (4%)
  starting transfers between devices  7.9 us (2%)
    all_gather x1, waiting for transfers between devices, on_device(): pairs = lax.all_gather(pairs, 'seq', axis=0, tiled=True)  131 us
    all_to_all x1, blocking collectives, on_device(): lax.all_to_all(outgoing, everywhere, split_axis=0, concat_axis=0, tiled=T...  121 us
    pallas_call x1, Pallas kernels, attention(): pl.pallas_call(attention_kernel, grid=(steps,), in_specs=[pl.BlockSpec(me...  40.3 us
    pallas_call x1, Pallas kernels, run_experts(): pl.pallas_call(functools.partial(experts_kernel, depth_steps=depth_steps)...  34.3 us
    pallas_call x1, Pallas kernels, combine(): pl.pallas_call(combine_kernel, grid=(width // FOLD,), in_specs=[pl.BlockS...  9.48 us
    pallas_call x1, Pallas kernels, dispatch(): pl.pallas_call(dispatch_kernel, grid=(4,), in_specs=[pl.BlockSpec(routed....  7.87 us
    all_to_all x1, starting transfers between devices, on_device(): lax.all_to_all(made, everywhere, split_axis=0, concat_axis=0, tiled=True)  7.67 us
  transfers between devices with their start and end apart: 2, of which 1 were waited for; matrix products, arithmetic and copies ran while one was open for 0% of the time, Pallas kernels for 11%

profile of v1, /device:TPU:39, one launch (start us, length us, event | category | flops | bytes accessed | tf_op | source)
XLA Modules:
  0.0 371.7 jit_solution(11450249322618403161)
XLA Ops:
  7.2 1.4 copy.10.routed_ref
  8.6 7.9 %dispatch_rows.1 = bf16[1024,4608]{1,0:T(8,128)(2,1)} custom-call(s32[128,8]{1,0:T(8,128)} %copy.10.routed_ref, bf16[128,4096]{1,0:T(8,128)(2,1)} %tokens_ref.1), custom_call_target="tpu_custom_call" | custom-call | flops 1207959552 | bytes 11000000 | tf_op jit(solution)/shard_map/dispatch_rows/pallas_call | solution.py:73
  16.4 121.3 %all_to_all.22 = bf16[128,8,4608]{2,1,0:T(8,128)(2,1)} all-to-all(bf16[128,8,4608]{2,1,0:T(8,128)(2,1)} %bitcast.9), channel_id=1, replica_groups=mesh['seq'=16,'exp'=8] {'seq','exp'}, dimensions={0} | all-to-all | bytes 18874368 | tf_op jit(solution)/shard_map/all_to_all | solution.py:287
  137.7 34.3 %run_experts.1 = bf16[1024,4608]{1,0:T(8,128)(2,1)} custom-call(bf16[1024,4608]{1,0:T(8,128)(2,1)} %bitcast.11, bf16[1024,4608]{1,0:T(8,128)(2,1)} %bitcast.12, bf16[1,4096,1536]{2,1,0:T(8,128)(2,1)} %up_ref.1, bf16[1,768,4096]{2,1,0:T(8,128)(2,1)} %down_ref.1), custom_call_target="tpu_custom_call" | custom-call | flops 21743271936 | bytes 38000000 | tf_op jit(solution)/shard_map/run_experts/pallas_call | solution.py:173
  172.0 0.0 copy-start
  172.0 0.0 copy-start.1
  172.1 0.0 copy-start.2
  172.1 7.7 %all-to-all-start.1 = ((bf16[128,8,4608]{2,1,0:T(8,128)(2,1)}), bf16[128,8,4608]{2,1,0:T(8,128)(2,1)}, u32[]{:S(2)}, u32[]{:S(2)}) async-start(bf16[128,8,4608]{2,1,0:T(8,128)(2,1)} %bitcast.10), calls=%async_computation.1 | async-start | bytes 18874368 | tf_op jit(solution)/shard_map/all_to_all | solution.py:291
  179.7 0.2 all-gather.2.cloned.1.call-start
  180.0 0.0 copy-done
  180.0 0.0 copy-done.1
  180.0 0.7 pad_maximum_fusion
  180.7 0.0 all-gather.2.cloned.1.call-update
  180.8 0.0 copy-done.2
  180.8 0.7 copy.12.gates_ref
  181.5 2.4 gate_matrix.1.gates_ref
  183.9 131.2 %all-gather.2.cloned.1.call-done.keys_ref.values_ref = bf16[2048,1024]{1,0:T(8,128)(2,1)} async-done(((bf16[128,1024]{1,0:T(8,128)(2,1)}), bf16[2048,1024]{1,0:T(8,128)(2,1)}) %all-gather.2.cloned.1.call-update) | async-done | bytes 4194320 | tf_op jit(solution)/shard_map/all_gather | solution.py:284
  315.1 40.3 %attention_rows.1 = bf16[128,8192]{1,0:T(8,128)(2,1)} custom-call(s32[1]{0:T(128)} %bitcast.first_ref, bf16[128,8192]{1,0:T(8,128)(2,1)} %bitcast.15, bf16[2048,1024]{1,0:T(8,128)(2,1)} %all-gather.2.cloned.1.call-done.keys_ref.values_ref, bf16[2048,1024]{1,0:T(8,128)(2,1)} %all-gather.2.cloned.1.call-done.keys_ref.values_ref), custom_call_target="tpu_custom_call" | custom-call | flops 8589934592 | bytes 9000000 | tf_op jit(solution)/shard_map/attention_rows/pallas_call | solution.py:263
  355.4 0.0 all-to-all-done.1
  355.4 9.5 %combine_rows.1 = bf16[128,4096]{1,0:T(8,128)(2,1)} custom-call(bf16[256,1152]{1,0:T(8,128)(2,1)} %gate_matrix.1.gates_ref, bf16[1024,4608]{1,0:T(8,128)(2,1)} %bitcast.8.rows_ref.last_ref, bf16[1024,4608]{1,0:T(8,128)(2,1)} %bitcast.8.rows_ref.last_ref), custom_call_target="tpu_custom_call" | custom-call | flops 2415919104 | bytes 11000000 | tf_op jit(solution)/shard_map/combine_rows/pallas_call | solution.py:219
Async XLA Ops:
  172.0 7.9 %copy-start = (bf16[1,128,512]{2,1,0:T(8,128)(2,1)S(1)}, bf16[1,128,512]{2,1,0:T(8,128)(2,1)}, u32[]{:S(2)}) copy-start(bf16[1,128,512]{2,1,0:T(8,128)(2,1)} %param.10) | copy-start | bytes 393220
  172.0 7.9 %copy-start.1 = (bf16[1,128,512]{2,1,0:T(8,128)(2,1)S(1)}, bf16[1,128,512]{2,1,0:T(8,128)(2,1)}, u32[]{:S(2)}) copy-start(bf16[1,128,512]{2,1,0:T(8,128)(2,1)} %param.9) | copy-start | bytes 393220
  172.1 8.7 %copy-start.2 = (f32[128,8]{0,1:T(8,128)S(1)}, f32[128,8]{0,1:T(8,128)}, u32[]{:S(2)}) copy-start(f32[128,8]{0,1:T(8,128)} %param.13) | copy-start | bytes 12292
  172.1 183.3 %all-to-all-start.1 = ((bf16[128,8,4608]{2,1,0:T(8,128)(2,1)}), bf16[128,8,4608]{2,1,0:T(8,128)(2,1)}, u32[]{:S(2)}, u32[]{:S(2)}) async-start(bf16[128,8,4608]{2,1,0:T(8,128)(2,1)} %bitcast.10), calls=%async_computation.1 | async-start | bytes 18874368 | tf_op jit(solution)/shard_map/all_to_all | solution.py:291
  179.7 135.4 %all-gather.2.cloned.1.call-start = ((), (), s32[]{:S(2)}) async-start(), calls=%async_computation.2 | async-start | bytes 4456448 | tf_op jit(solution)/shard_map/all_gather | solution.py:284
Sparse Core Ops, SparseCore 0:
  182.9 132.2 all-gather.1

commit v2 on v1

v2 whole, which is shorter than its diff:
```python
import functools

import jax
import jax.numpy as jnp
from jax import lax
from jax.experimental import pallas as pl
from jax.experimental.pallas import tpu as pltpu
from jax.sharding import PartitionSpec as P

HEAD_SIZE = 128
BAND = 8
FOLD = 512
BF = jnp.bfloat16
F32 = jnp.float32
VMEM = 56 * 1024 * 1024


def iota(shape, dim):
    return lax.broadcasted_iota(jnp.int32, shape, dim)


def dot(a, b):
    return jnp.dot(a, b, preferred_element_type=F32)


def fold_matrix():
    row, col = iota((256, 256), 0), iota((256, 256), 1)
    return (col == (row & 7) * 32 + (row >> 3)).astype(F32).astype(BF)


def unfold_matrix():
    row, col = iota((256, 256), 0), iota((256, 256), 1)
    return (col == (row & 31) * 8 + (row >> 5)).astype(F32).astype(BF)


def ranks(routed):
    tokens = routed.shape[1]
    experts = iota((128, tokens), 0)
    named = jnp.zeros((128, tokens), F32)
    for j in range(routed.shape[0]):
        named = jnp.where(routed[j : j + 1, :] == experts, 1.0, named)
    earlier = (iota((tokens, tokens), 0) < iota((tokens, tokens), 1)).astype(F32).astype(BF)
    before = dot(named.astype(BF), earlier)
    return jnp.where(named > 0.5, before, -1.0)


def send_block(rows_ref, fold_ref, out_hbm, sems, b):
    width = rows_ref.shape[1]
    rows = pl.ds(b * 256, 256)
    copies = [
        pltpu.make_async_copy(
            rows_ref.at[pl.ds(b * 288, 256), :], out_hbm.at[rows, pl.ds(0, width)], sems.at[b, 0]
        ),
        pltpu.make_async_copy(fold_ref.at[rows, :], out_hbm.at[rows, pl.ds(width, FOLD)], sems.at[b, 1]),
    ]
    copies[0].start()
    ninth = slice(b * 288 + 256, (b + 1) * 288)
    piece = jnp.concatenate([rows_ref[ninth, r * FOLD : (r + 1) * FOLD] for r in range(8)], axis=0)
    fold_ref[b * 256 : (b + 1) * 256, :] = dot(fold_matrix(), piece).astype(BF)
    copies[1].start()
    return copies


def dispatch_kernel(routed_ref, tokens_hbm, out_hbm, tokens_ref, rows_ref, fold_ref, in_sem, sems):
    width = tokens_ref.shape[1]
    load = pltpu.make_async_copy(tokens_hbm, tokens_ref, in_sem.at[0])
    load.start()
    rank = ranks(routed_ref[...])
    low = rank.astype(BF)
    copies = []
    for b in range(4):
        expand = (iota((256, 128), 1) == b * 32 + (iota((256, 128), 0) >> 3)).astype(F32).astype(BF)
        band = dot(expand, low) == (iota((256, 128), 0) & 7).astype(F32)
        ninth = rank[b * 32 : (b + 1) * 32] == float(BAND)
        pick = jnp.concatenate([jnp.where(band, 1.0, 0.0), jnp.where(ninth, 1.0, 0.0)], axis=0).astype(BF)
        if b == 0:
            load.wait()
        for c in range(width // FOLD):
            cols = slice(c * FOLD, (c + 1) * FOLD)
            rows_ref[b * 288 : (b + 1) * 288, cols] = dot(pick, tokens_ref[:, cols]).astype(BF)
        copies += send_block(rows_ref, fold_ref, out_hbm, sems, b)
    for copy in copies:
        copy.wait()


def dispatch(routed, tokens):
    width = tokens.shape[1]
    return pl.pallas_call(
        dispatch_kernel,
        in_specs=[pl.BlockSpec(memory_space=pltpu.VMEM), pl.BlockSpec(memory_space=pl.ANY)],
        out_specs=pl.BlockSpec(memory_space=pl.ANY),
        out_shape=jax.ShapeDtypeStruct((128 * BAND, width + FOLD), BF),
        scratch_shapes=[
            pltpu.VMEM(tokens.shape, BF),
            pltpu.VMEM((4 * 288, width), BF),
            pltpu.VMEM((1024, FOLD), BF),
            pltpu.SemaphoreType.DMA((1,)),
            pltpu.SemaphoreType.DMA((4, 2)),
        ],
        compiler_params=pltpu.CompilerParams(vmem_limit_bytes=VMEM),
        cost_estimate=pl.CostEstimate(flops=2 * 1152 * 128 * 4096, bytes_accessed=11_000_000, transcendentals=0),
        name="dispatch_rows",
    )(routed, tokens)


def gates_kernel(routed_ref, gates_ref, out_ref):
    routed = routed_ref[...]
    tokens = routed.shape[1]
    rank = ranks(routed)
    experts = iota((128, tokens), 0)
    gate = jnp.zeros((128, tokens), F32)
    for j in range(routed.shape[0]):
        gate = jnp.where(routed[j : j + 1, :] == experts, gates_ref[j : j + 1, :], gate)
    gate = gate.T
    rank = rank.T
    high = gate.astype(BF)
    low = (gate - high.astype(F32)).astype(BF)
    wide = 128 * BAND
    expand = (iota((128, wide), 0) == (iota((128, wide), 1) >> 3)).astype(F32).astype(BF)
    chosen = dot(rank.astype(BF), expand) == (iota((tokens, wide), 1) & 7).astype(F32)
    for part, value in enumerate((high, low)):
        rows = slice(part * tokens, (part + 1) * tokens)
        out_ref[rows, :wide] = jnp.where(chosen, dot(value, expand), 0.0).astype(BF)
        out_ref[rows, wide:] = jnp.where(rank == float(BAND), value.astype(F32), 0.0).astype(BF)


def gate_matrix(routed, gates):
    tokens = routed.shape[1]
    return pl.pallas_call(
        gates_kernel,
        out_shape=jax.ShapeDtypeStruct((2 * tokens, 128 * (BAND + 1)), BF),
        compiler_params=pltpu.CompilerParams(vmem_limit_bytes=VMEM),
        cost_estimate=pl.CostEstimate(flops=6 * 128 * 128 * 1024, bytes_accessed=700_000, transcendentals=0),
        name="gate_matrix",
    )(routed, gates)


def experts_kernel(
    rows_hbm, up_hbm, down_hbm, out_hbm,
    rows_ref, last_ref, up_ref, down_ref, sum_ref, hidden_ref, made_ref, fold_ref,
    row_sems, up_sems, down_sems, sems,
    *, deep, part, wide,
):
    width = rows_ref.shape[1]
    units = hidden_ref.shape[1]
    chunks = width // deep

    def load_rows(b):
        rows = pl.ds(b * 256, 256)
        return [
            pltpu.make_async_copy(rows_hbm.at[rows, pl.ds(width, FOLD)], last_ref.at[rows, :], row_sems.at[b, 0]),
            pltpu.make_async_copy(
                rows_hbm.at[rows, pl.ds(0, width)], rows_ref.at[pl.ds(b * 288, 256), :], row_sems.at[b, 1]
            ),
        ]

    def load_up(k):
        rows = pl.ds(k * deep, deep)
        return pltpu.make_async_copy(up_hbm.at[0, rows, :], up_ref.at[rows, :], up_sems.at[k])

    def load_down(k):
        rows = pl.ds(k * 256, 256)
        return pltpu.make_async_copy(down_hbm.at[0, rows, :], down_ref.at[rows, :], down_sems.at[k])

    row_loads = [load_rows(b) for b in range(4)]
    up_loads = [load_up(k) for k in range(chunks)]
    down_loads = [load_down(k) for k in range(units // 256)]
    later = row_loads[1] + row_loads[2] + row_loads[3] + down_loads
    for load in row_loads[0] + up_loads:
        load.start()

    def ready(b):
        for load in row_loads[b]:
            load.wait()
        piece = dot(unfold_matrix(), last_ref[b * 256 : (b + 1) * 256, :]).astype(BF)
        for r in range(8):
            rows_ref[b * 288 + 256 : (b + 1) * 288, r * FOLD : (r + 1) * FOLD] = piece[r * 32 : (r + 1) * 32]

    def activate(gate, linear):
        return (gate / (1.0 + jnp.exp(-gate)) * linear).astype(BF)

    ready(0)
    for k in range(chunks):
        up_loads[k].wait()
        cols = slice(k * deep, (k + 1) * deep)
        term = dot(rows_ref[:288, cols], up_ref[cols, :])
        if k == 0:
            sum_ref[...] = term
        elif k < chunks - 1:
            sum_ref[...] += term
        else:
            term = sum_ref[...] + term
            hidden_ref[:288, :] = activate(term[:, :units], term[:, units:])
        count = -(-len(later) // chunks)
        for load in later[k * count : (k + 1) * count]:
            load.start()
    for first, last in ((1, 2), (2, 4)):
        for b in range(first, last):
            ready(b)
        rows = slice(first * 288, last * 288)
        for c in range(units // part):
            cols = slice(c * part, (c + 1) * part)
            gate = dot(rows_ref[rows, :], up_ref[:, cols])
            linear = dot(rows_ref[rows, :], up_ref[:, units + c * part : units + (c + 1) * part])
            hidden_ref[rows, cols] = activate(gate, linear)
    for load in down_loads:
        load.wait()
    copies = []
    for first, last in ((0, 2), (2, 4)):
        rows = slice(first * 288, last * 288)
        for c in range(width // wide):
            cols = slice(c * wide, (c + 1) * wide)
            made_ref[rows, cols] = dot(hidden_ref[rows, :], down_ref[:, cols]).astype(BF)
        for b in range(first, last):
            copies += send_block(made_ref, fold_ref, out_hbm, sems, b)
    for copy in copies:
        copy.wait()


def run_experts(arrived, up, down, deep=1024, part=256, wide=512):
    rows = arrived.shape[0]
    width = up.shape[1]
    units = down.shape[1]
    all_rows = rows + 128
    return pl.pallas_call(
        functools.partial(experts_kernel, deep=deep, part=part, wide=wide),
        in_specs=[pl.BlockSpec(memory_space=pl.ANY)] * 3,
        out_specs=pl.BlockSpec(memory_space=pl.ANY),
        out_shape=jax.ShapeDtypeStruct(arrived.shape, BF),
        scratch_shapes=[
            pltpu.VMEM((all_rows, width), BF),
            pltpu.VMEM((rows, FOLD), BF),
            pltpu.VMEM((width, 2 * units), BF),
            pltpu.VMEM((units, width), BF),
            pltpu.VMEM((288, 2 * units), F32),
            pltpu.VMEM((all_rows, units), BF),
            pltpu.VMEM((all_rows, width), BF),
            pltpu.VMEM((rows, FOLD), BF),
            pltpu.SemaphoreType.DMA((4, 2)),
            pltpu.SemaphoreType.DMA((width // deep,)),
            pltpu.SemaphoreType.DMA((units // 256,)),
            pltpu.SemaphoreType.DMA((4, 2)),
        ],
        compiler_params=pltpu.CompilerParams(vmem_limit_bytes=VMEM),
        cost_estimate=pl.CostEstimate(
            flops=2 * all_rows * units * 3 * width, bytes_accessed=38_000_000, transcendentals=all_rows * units
        ),
        name="run_experts",
    )(arrived, up, down)


def combine_kernel(gates_ref, rows_hbm, out_hbm, rows_ref, ninth_ref, sum_ref, out_ref, in_sems, sem):
    tokens, width = out_ref.shape
    wide = rows_ref.shape[0]
    loads = [
        pltpu.make_async_copy(rows_hbm.at[pl.ds(b * 128, 128), :], rows_ref.at[pl.ds(b * 128, 128), :], in_sems.at[b])
        for b in range(wide // 128)
    ]
    for load in loads:
        load.start()
    unfold = unfold_matrix()
    for half in range(2):
        for b in range(half * 4, half * 4 + 4):
            loads[b].wait()
        for b in range(half * 2, half * 2 + 2):
            piece = dot(unfold, rows_ref[b * 256 : (b + 1) * 256, width:]).astype(BF)
            for r in range(8):
                ninth_ref[r, b * 32 : (b + 1) * 32, :] = piece[r * 32 : (r + 1) * 32]
        rows = slice(half * 512, (half + 1) * 512)
        for c in range(width // FOLD):
            cols = slice(c * FOLD, (c + 1) * FOLD)
            both = dot(gates_ref[:, rows], rows_ref[rows, cols])
            if half == 0:
                sum_ref[:, cols] = both[:tokens] + both[tokens:]
            else:
                both += dot(gates_ref[:, wide:], ninth_ref[c])
                out_ref[:, cols] = (sum_ref[:, cols] + both[:tokens] + both[tokens:]).astype(BF)
    copy = pltpu.make_async_copy(out_ref, out_hbm, sem.at[0])
    copy.start()
    copy.wait()


def combine(gates, returned):
    rows = returned.shape[0]
    width = returned.shape[1] - FOLD
    tokens = gates.shape[0] // 2
    return pl.pallas_call(
        combine_kernel,
        in_specs=[pl.BlockSpec(memory_space=pltpu.VMEM), pl.BlockSpec(memory_space=pl.ANY)],
        out_specs=pl.BlockSpec(memory_space=pl.ANY),
        out_shape=jax.ShapeDtypeStruct((tokens, width), BF),
        scratch_shapes=[
            pltpu.VMEM(returned.shape, BF),
            pltpu.VMEM((8, 128, FOLD), BF),
            pltpu.VMEM((tokens, width), F32),
            pltpu.VMEM((tokens, width), BF),
            pltpu.SemaphoreType.DMA((rows // 128,)),
            pltpu.SemaphoreType.DMA((1,)),
        ],
        compiler_params=pltpu.CompilerParams(vmem_limit_bytes=VMEM),
        cost_estimate=pl.CostEstimate(flops=2 * 256 * 1152 * 4096, bytes_accessed=11_000_000, transcendentals=0),
        name="combine_rows",
    )(gates, returned)


def attention_kernel(first_ref, queries_ref, keys_ref, values_ref, out_ref):
    rows = queries_ref.shape[0]
    length = keys_ref.shape[0]
    heads = queries_ref.shape[1] // HEAD_SIZE
    position = first_ref[0] + iota((rows, length), 0)
    seen = iota((rows, length), 1) <= position
    factor = HEAD_SIZE**-0.5 * 1.4426950408889634
    for h in range(heads):
        cols = slice(h * HEAD_SIZE, (h + 1) * HEAD_SIZE)
        scores = lax.dot_general(
            queries_ref[:, cols], keys_ref[...], (((1,), (1,)), ((), ())), preferred_element_type=F32
        )
        scores = jnp.where(seen, scores, -1e30)
        top = jnp.max(scores, axis=-1, keepdims=True)
        part = jnp.exp2((scores - top) * factor)
        total = jnp.sum(part, axis=-1, keepdims=True)
        mixed = dot(part.astype(BF), values_ref[...])
        out_ref[:, cols] = (mixed / total).astype(BF)


def attention(first, queries, pairs, heads_per_step=16):
    rows, width = queries.shape
    length = pairs.shape[0]
    kv_heads = pairs.shape[1] // (2 * HEAD_SIZE)
    steps = width // (heads_per_step * HEAD_SIZE)
    per_kv = steps // kv_heads
    block = (rows, heads_per_step * HEAD_SIZE)
    return pl.pallas_call(
        attention_kernel,
        grid=(steps,),
        in_specs=[
            pl.BlockSpec(memory_space=pltpu.SMEM),
            pl.BlockSpec(block, lambda i: (0, i)),
            pl.BlockSpec((length, HEAD_SIZE), lambda i: (0, i // per_kv)),
            pl.BlockSpec((length, HEAD_SIZE), lambda i: (0, kv_heads + i // per_kv)),
        ],
        out_specs=pl.BlockSpec(block, lambda i: (0, i)),
        out_shape=jax.ShapeDtypeStruct(queries.shape, BF),
        compiler_params=pltpu.CompilerParams(vmem_limit_bytes=VMEM),
        cost_estimate=pl.CostEstimate(
            flops=4 * rows * width * length, bytes_accessed=9_000_000, transcendentals=rows * length * width // HEAD_SIZE
        ),
        name="attention_rows",
    )(first, queries, pairs, pairs)


def on_device(queries, keys, values, tokens, routed, gates, up, down):
    pairs = jnp.concatenate([keys[0], values[0]], axis=1)
    pairs = lax.all_gather(pairs, "seq", axis=0, tiled=True)
    everywhere = ("seq", "exp")
    outgoing = dispatch(routed.T, tokens)
    arrived = lax.all_to_all(outgoing, everywhere, split_axis=0, concat_axis=0, tiled=True)
    arrived, pairs = lax.optimization_barrier((arrived, pairs))
    made = run_experts(arrived, up, down)
    made, own, routed, gates = lax.optimization_barrier((made, queries[0], routed, gates))
    returned = lax.all_to_all(made, everywhere, split_axis=0, concat_axis=0, tiled=True)
    weights = gate_matrix(routed.T, gates.T)
    first = (lax.axis_index("seq") * own.shape[0]).astype(jnp.int32).reshape(1)
    attended = attention(first, own, pairs)
    return (attended[None], combine(weights, returned))


def solution(mesh):
    spread = P(("seq", "exp"), None)
    in_specs = (P("exp", "seq", None),) * 3 + (spread,) * 3 + (P(("seq", "exp"), None, None),) * 2
    out_specs = (P("exp", "seq", None), spread)
    return jax.shard_map(on_device, mesh=mesh, in_specs=in_specs, out_specs=out_specs, check_vma=False)
```

time: 378 us -> 355 us (0.939)
  blocking collectives: 121 us -> 0 us
  waiting for transfers between devices: 131 us -> 232 us
  Pallas kernels: 94.4 us -> 83.2 us
  starting transfers between devices: 7.9 us -> 18.7 us
    all_to_all x1 -> x0, blocking collectives: 121 us -> none  [on_device(): lax.all_to_all(outgoing, everywhere, split_axis=0, concat_axis=0, tiled=T...]
    all_to_all x1, waiting for transfers between devices: 0.01 us -> 90 us  [on_device(): lax.all_to_all(made, everywhere, split_axis=0, concat_axis=0, tiled=True)]
    all_to_all x0 -> x1, starting transfers between devices: none -> 10.9 us  [on_device(): lax.all_to_all(outgoing, everywhere, split_axis=0, concat_axis=0, tiled=T...]
    all_to_all x0 -> x1, waiting for transfers between devices: none -> 7.44 us  [on_device(): lax.all_to_all(outgoing, everywhere, split_axis=0, concat_axis=0, tiled=T...]
    pallas_call x3, Pallas kernels: 51.7 us -> 45.6 us  [the longest x1 30.7 us: run_experts(): pl.pallas_call(functools.partial(experts_kernel, deep=deep, part=part, wi...]
    pallas_call x1, Pallas kernels: 40.3 us -> 35.4 us  [attention(): pl.pallas_call(attention_kernel, grid=(steps,), in_specs=[pl.BlockSpec(me...]
  transfers between devices with their start and end apart: 2 -> 3, of which waited for: 1 -> 3; matrix products, arithmetic and copies ran while one was open for 0% -> 0% of each run, Pallas kernels for 11% -> 11%
where the time goes in v2:
time: 355 us; the launch traced here: 349 us
  waiting for transfers between devices  232 us (65%)
  Pallas kernels  83.2 us (23%)
  starting transfers between devices  18.7 us (5%)
  between operations  14.1 us (4%)
    all_gather x1, waiting for transfers between devices, on_device(): pairs = lax.all_gather(pairs, 'seq', axis=0, tiled=True)  134 us
    all_to_all x1, waiting for transfers between devices, on_device(): lax.all_to_all(made, everywhere, split_axis=0, concat_axis=0, tiled=True)  90 us
    pallas_call x1, Pallas kernels, attention(): pl.pallas_call(attention_kernel, grid=(steps,), in_specs=[pl.BlockSpec(me...  35.4 us
    pallas_call x1, Pallas kernels, run_experts(): pl.pallas_call(functools.partial(experts_kernel, deep=deep, part=part, wi...  30.7 us
    all_to_all x1, starting transfers between devices, on_device(): lax.all_to_all(outgoing, everywhere, split_axis=0, concat_axis=0, tiled=T...  10.9 us
    pallas_call x1, Pallas kernels, combine(): pl.pallas_call(combine_kernel, in_specs=[pl.BlockSpec(memory_space=pltpu....  7.85 us
    all_to_all x1, starting transfers between devices, on_device(): lax.all_to_all(made, everywhere, split_axis=0, concat_axis=0, tiled=True)  7.56 us
    all_to_all x1, waiting for transfers between devices, on_device(): lax.all_to_all(outgoing, everywhere, split_axis=0, concat_axis=0, tiled=T...  7.44 us
  transfers between devices with their start and end apart: 3, of which 3 were waited for; matrix products, arithmetic and copies ran while one was open for 0% of the time, Pallas kernels for 11%

profile of v2, /device:TPU:39, one launch (start us, length us, event | category | flops | bytes accessed | tf_op | source)
XLA Modules:
  0.0 348.6 jit_solution(8933153938513976074)
XLA Ops:
  7.2 7.1 %dispatch_rows.1 = bf16[1024,4608]{1,0:T(8,128)(2,1)} custom-call(s32[8,128]{1,0:T(8,128)} %bitcast.16, bf16[128,4096]{1,0:T(8,128)(2,1)} %tokens_hbm.1), custom_call_target="tpu_custom_call" | custom-call | flops 1207959552 | bytes 11000000 | tf_op jit(solution)/shard_map/dispatch_rows/pallas_call | solution.py:88
  14.2 0.0 copy-start
  14.2 0.0 copy-start.1
  14.2 10.9 %all-to-all-start = ((bf16[128,8,4608]{2,1,0:T(8,128)(2,1)}), bf16[128,8,4608]{2,1,0:T(8,128)(2,1)}, u32[]{:S(2)}, u32[]{:S(2)}) async-start(bf16[128,8,4608]{2,1,0:T(8,128)(2,1)} %bitcast.12), calls=%async_computation | async-start | bytes 18874368 | tf_op jit(solution)/shard_map/all_to_all | solution.py:357
  25.2 0.2 all-gather.2.cloned.1.call-start
  25.4 0.0 copy-done
  25.4 0.0 copy-done.1
  25.4 0.7 pad_maximum_fusion
  26.1 0.0 all-gather.2.cloned.1.call-update
  26.2 134.4 %all-gather.2.cloned.1.call-done.keys_ref.values_ref = bf16[2048,1024]{1,0:T(8,128)(2,1)} async-done(((bf16[128,1024]{1,0:T(8,128)(2,1)}), bf16[2048,1024]{1,0:T(8,128)(2,1)}) %all-gather.2.cloned.1.call-update) | async-done | bytes 4194320 | tf_op jit(solution)/shard_map/all_gather | solution.py:354
  160.6 7.4 %all-to-all-done = bf16[128,8,4608]{2,1,0:T(8,128)(2,1)} async-done(((bf16[128,8,4608]{2,1,0:T(8,128)(2,1)}), bf16[128,8,4608]{2,1,0:T(8,128)(2,1)}, u32[]{:S(2)}, u32[]{:S(2)}) %all-to-all-start) | async-done | bytes 9437216 | tf_op jit(solution)/shard_map/all_to_all | solution.py:357
  168.0 30.7 %run_experts.1 = bf16[1024,4608]{1,0:T(8,128)(2,1)} custom-call(bf16[1024,4608]{1,0:T(8,128)(2,1)} %bitcast.3.rows_hbm, bf16[1,4096,1536]{2,1,0:T(8,128)(2,1)} %up_hbm.1, bf16[1,768,4096]{2,1,0:T(8,128)(2,1)} %down_hbm.1), custom_call_target="tpu_custom_call" | custom-call | flops 21743271936 | bytes 38000000 | tf_op jit(solution)/shard_map/run_experts/pallas_call | solution.py:225
  198.7 7.6 %all-to-all-start.1 = ((bf16[128,8,4608]{2,1,0:T(8,128)(2,1)}), bf16[128,8,4608]{2,1,0:T(8,128)(2,1)}, u32[]{:S(2)}, u32[]{:S(2)}) async-start(bf16[128,8,4608]{2,1,0:T(8,128)(2,1)} %bitcast.13), calls=%async_computation.1 | async-start | bytes 18874368 | tf_op jit(solution)/shard_map/all_to_all | solution.py:361
  206.3 2.1 gate_matrix.1.gates_ref
  208.4 35.4 %attention_rows.1 = bf16[128,8192]{1,0:T(8,128)(2,1)} custom-call(s32[1]{0:T(128)} %bitcast.first_ref, bf16[128,8192]{1,0:T(8,128)(2,1)} %bitcast.19, bf16[2048,1024]{1,0:T(8,128)(2,1)} %all-gather.2.cloned.1.call-done.keys_ref.values_ref, bf16[2048,1024]{1,0:T(8,128)(2,1)} %all-gather.2.cloned.1.call-done.keys_ref.values_ref), custom_call_target="tpu_custom_call" | custom-call | flops 8589934592 | bytes 9000000 | tf_op jit(solution)/shard_map/attention_rows/pallas_call | solution.py:333
  243.8 90.0 %all-to-all-done.1 = bf16[128,8,4608]{2,1,0:T(8,128)(2,1)} async-done(((bf16[128,8,4608]{2,1,0:T(8,128)(2,1)}), bf16[128,8,4608]{2,1,0:T(8,128)(2,1)}, u32[]{:S(2)}, u32[]{:S(2)}) %all-to-all-start.1) | async-done | bytes 9437216 | tf_op jit(solution)/shard_map/all_to_all | solution.py:361
  333.9 7.8 %combine_rows.1 = bf16[128,4096]{1,0:T(8,128)(2,1)} custom-call(bf16[256,1152]{1,0:T(8,128)(2,1)} %gate_matrix.1.gates_ref, bf16[1024,4608]{1,0:T(8,128)(2,1)} %bitcast.11.rows_hbm), custom_call_target="tpu_custom_call" | custom-call | flops 2415919104 | bytes 11000000 | tf_op jit(solution)/shard_map/combine_rows/pallas_call | solution.py:287
Async XLA Ops:
  14.2 11.2 %copy-start = (bf16[1,128,512]{2,1,0:T(8,128)(2,1)S(1)}, bf16[1,128,512]{2,1,0:T(8,128)(2,1)}, u32[]{:S(2)}) copy-start(bf16[1,128,512]{2,1,0:T(8,128)(2,1)} %param.10) | copy-start | bytes 393220
  14.2 11.2 %copy-start.1 = (bf16[1,128,512]{2,1,0:T(8,128)(2,1)S(1)}, bf16[1,128,512]{2,1,0:T(8,128)(2,1)}, u32[]{:S(2)}) copy-start(bf16[1,128,512]{2,1,0:T(8,128)(2,1)} %param.9) | copy-start | bytes 393220
  14.2 153.7 %all-to-all-start = ((bf16[128,8,4608]{2,1,0:T(8,128)(2,1)}), bf16[128,8,4608]{2,1,0:T(8,128)(2,1)}, u32[]{:S(2)}, u32[]{:S(2)}) async-start(bf16[128,8,4608]{2,1,0:T(8,128)(2,1)} %bitcast.12), calls=%async_computation | async-start | bytes 18874368 | tf_op jit(solution)/shard_map/all_to_all | solution.py:357
  25.2 135.4 %all-gather.2.cloned.1.call-start = ((), (), s32[]{:S(2)}) async-start(), calls=%async_computation.2 | async-start | bytes 4456448 | tf_op jit(solution)/shard_map/all_gather | solution.py:354
  198.7 135.2 %all-to-all-start.1 = ((bf16[128,8,4608]{2,1,0:T(8,128)(2,1)}), bf16[128,8,4608]{2,1,0:T(8,128)(2,1)}, u32[]{:S(2)}, u32[]{:S(2)}) async-start(bf16[128,8,4608]{2,1,0:T(8,128)(2,1)} %bitcast.13), calls=%async_computation.1 | async-start | bytes 18874368 | tf_op jit(solution)/shard_map/all_to_all | solution.py:361
Sparse Core Ops, SparseCore 0:
  28.3 132.2 all-gather.1

commit v3 on v2

v3 whole, which is shorter than its diff:
```python
import functools

import jax
import jax.numpy as jnp
from jax import lax
from jax.experimental import pallas as pl
from jax.experimental.pallas import tpu as pltpu
from jax.sharding import PartitionSpec as P

HEAD_SIZE = 128
HALF = 4
LAST = 8
FOLD = 512
BF = jnp.bfloat16
F32 = jnp.float32
VMEM = 56 * 1024 * 1024


def iota(shape, dim):
    return lax.broadcasted_iota(jnp.int32, shape, dim)


def dot(a, b):
    return jnp.dot(a, b, preferred_element_type=F32)


def permutation(source):
    row, col = iota((256, 256), 0), iota((256, 256), 1)
    return (col == source(row)).astype(F32).astype(BF)


def fold_matrix():
    return permutation(lambda i: (i & 7) * 32 + (i >> 3))


def unfold_matrix():
    return permutation(lambda i: (i & 31) * 8 + (i >> 5))


def fold_half_matrix():
    return permutation(lambda i: ((i >> 2) & 1) * 128 + (i >> 3) * 4 + (i & 3))


def unfold_half_matrix():
    return permutation(lambda i: ((i >> 2) & 31) * 8 + (i >> 7) * 4 + (i & 3))


def ranks(routed):
    tokens = routed.shape[1]
    experts = iota((128, tokens), 0)
    named = jnp.zeros((128, tokens), F32)
    for j in range(routed.shape[0]):
        named = jnp.where(routed[j : j + 1, :] == experts, 1.0, named)
    earlier = (iota((tokens, tokens), 0) < iota((tokens, tokens), 1)).astype(F32).astype(BF)
    before = dot(named.astype(BF), earlier)
    return jnp.where(named > 0.5, before, -1.0)


def block_copy(source, target, b, columns, sem):
    rows = pl.ds(b * 256, 256)
    return pltpu.make_async_copy(source.at[rows, :], target.at[rows, columns], sem)


def dispatch_kernel(
    routed_ref, tokens_hbm, out_hbm, tokens_ref, rows_ref, ninth_ref, fold_ref, in_sems, sems, *, first, ninth
):
    half = tokens_ref.shape[1]
    parts = half // FOLD
    loads = [
        pltpu.make_async_copy(
            tokens_hbm.at[:, pl.ds(h * half, half)], tokens_ref.at[pl.ds(h * 128, 128), :], in_sems.at[h]
        )
        for h in range(2)
    ]
    for load in loads:
        load.start()
    rank = ranks(routed_ref[...])
    low = rank.astype(BF)
    row = iota((256, 128), 0)
    slot = ((row & 3) + first).astype(F32)
    upper = ((row >> 2) & 1) == 1
    copies = []
    for b in range(4):
        expand = (iota((256, 128), 1) == b * 32 + (row >> 3)).astype(F32).astype(BF)
        band = jnp.where(dot(expand, low) == slot, 1.0, 0.0)
        pick = jnp.concatenate([jnp.where(upper, 0.0, band), jnp.where(upper, band, 0.0)], axis=1).astype(BF)
        if b == 0:
            for load in loads:
                load.wait()
        for c in range(parts):
            cols = slice(c * FOLD, (c + 1) * FOLD)
            rows_ref[b * 256 : (b + 1) * 256, cols] = dot(pick, tokens_ref[:, cols]).astype(BF)
        copies.append(block_copy(rows_ref, out_hbm, b, pl.ds(0, half), sems.at[b, 0]))
        copies[-1].start()
    if ninth:
        pick = jnp.where(rank == float(LAST), 1.0, 0.0).astype(BF)
        for r in range(2 * parts):
            h, c = divmod(r, parts)
            ninth_ref[r] = dot(pick, tokens_ref[h * 128 : (h + 1) * 128, c * FOLD : (c + 1) * FOLD]).astype(BF)
        fold = fold_matrix()
        for b in range(4):
            piece = jnp.concatenate([ninth_ref[r, b * 32 : (b + 1) * 32, :] for r in range(8)], axis=0)
            fold_ref[b * 256 : (b + 1) * 256, :] = dot(fold, piece).astype(BF)
            copies.append(block_copy(fold_ref, out_hbm, b, pl.ds(half, FOLD), sems.at[b, 1]))
            copies[-1].start()
    for copy in copies:
        copy.wait()


def dispatch(routed, tokens, second):
    half = tokens.shape[1] // 2
    return pl.pallas_call(
        functools.partial(dispatch_kernel, first=HALF * second, ninth=second),
        in_specs=[pl.BlockSpec(memory_space=pltpu.VMEM), pl.BlockSpec(memory_space=pl.ANY)],
        out_specs=pl.BlockSpec(memory_space=pl.ANY),
        out_shape=jax.ShapeDtypeStruct((1024, half + FOLD * second), BF),
        scratch_shapes=[
            pltpu.VMEM((256, half), BF),
            pltpu.VMEM((1024, half), BF),
            pltpu.VMEM((8, 128, FOLD), BF),
            pltpu.VMEM((1024, FOLD), BF),
            pltpu.SemaphoreType.DMA((2,)),
            pltpu.SemaphoreType.DMA((4, 2)),
        ],
        compiler_params=pltpu.CompilerParams(vmem_limit_bytes=VMEM),
        cost_estimate=pl.CostEstimate(flops=2 * 640 * 128 * 4096, bytes_accessed=6_000_000, transcendentals=0),
        name="dispatch_rows",
    )(routed, tokens)


def gates_kernel(routed_ref, gates_ref, first_ref, second_ref, ninth_ref):
    routed = routed_ref[...]
    tokens = routed.shape[1]
    rank = ranks(routed)
    experts = iota((128, tokens), 0)
    gate = jnp.zeros((128, tokens), F32)
    for j in range(routed.shape[0]):
        gate = jnp.where(routed[j : j + 1, :] == experts, gates_ref[j : j + 1, :], gate)
    gate = gate.T
    rank = rank.T
    high = gate.astype(BF)
    low = (gate - high.astype(F32)).astype(BF)
    expand = (iota((128, 1024), 0) == (iota((128, 1024), 1) >> 3)).astype(F32).astype(BF)
    spread = dot(rank.astype(BF), expand)
    lane = iota((tokens, 1024), 1)
    slot = (lane & 3).astype(F32)
    for part, value in enumerate((high, low)):
        wide = dot(value, expand)
        ninth_ref[part * tokens : (part + 1) * tokens, :] = jnp.where(
            rank == float(LAST), value.astype(F32), 0.0
        ).astype(BF)
        for h in range(2):
            rows = slice((part * 2 + h) * tokens, (part * 2 + h + 1) * tokens)
            kept = jnp.where(((lane >> 2) & 1) == h, wide, 0.0)
            first_ref[rows, :] = jnp.where(spread == slot, kept, 0.0).astype(BF)
            second_ref[rows, :] = jnp.where(spread == slot + float(HALF), kept, 0.0).astype(BF)


def gate_matrices(routed, gates):
    tokens = routed.shape[1]
    shape = jax.ShapeDtypeStruct((4 * tokens, 1024), BF)
    return pl.pallas_call(
        gates_kernel,
        out_shape=(shape, shape, jax.ShapeDtypeStruct((2 * tokens, 128), BF)),
        compiler_params=pltpu.CompilerParams(vmem_limit_bytes=VMEM),
        cost_estimate=pl.CostEstimate(flops=6 * 128 * 128 * 1024, bytes_accessed=2_200_000, transcendentals=0),
        name="gate_matrices",
    )(routed, gates)


def experts_kernel(
    rows_hbm, up_hbm, down_hbm, out_hbm,
    stage_ref, last_ref, rows_ref, up_ref, down_ref, hidden_ref, made_ref, sent_ref, fold_ref,
    row_sems, up_sems, down_sems, sems,
    *, ninth, part,
):
    half = stage_ref.shape[1]
    width = rows_ref.shape[1]
    units = hidden_ref.shape[1]
    count = rows_ref.shape[0] // 4
    parts = half // FOLD
    chunks = up_sems.shape[0]
    deep = width // chunks

    row_loads = []
    for b in range(4):
        rows = pl.ds(b * 256, 256)
        loads = [pltpu.make_async_copy(rows_hbm.at[rows, pl.ds(0, half)], stage_ref.at[rows, :], row_sems.at[b, 0])]
        if ninth:
            loads.append(
                pltpu.make_async_copy(rows_hbm.at[rows, pl.ds(half, FOLD)], last_ref.at[rows, :], row_sems.at[b, 1])
            )
        row_loads.append(loads)
    up_loads = [
        pltpu.make_async_copy(
            up_hbm.at[0, pl.ds(k * deep, deep), :], up_ref.at[pl.ds(k * deep, deep), :], up_sems.at[k]
        )
        for k in range(chunks)
    ]
    down_load = pltpu.make_async_copy(down_hbm.at[0], down_ref, down_sems.at[0])
    for loads in row_loads:
        for load in loads:
            load.start()
    for load in up_loads:
        load.start()
    down_load.start()

    unfold_half = unfold_half_matrix()
    for b in range(4):
        for load in row_loads[b]:
            load.wait()
        for c in range(parts):
            cols = slice(c * FOLD, (c + 1) * FOLD)
            both = dot(unfold_half, stage_ref[b * 256 : (b + 1) * 256, cols]).astype(BF)
            rows_ref[b * count : b * count + 128, cols] = both[:128]
            rows_ref[b * count : b * count + 128, half + c * FOLD : half + (c + 1) * FOLD] = both[128:]
        if ninth:
            piece = dot(unfold_matrix(), last_ref[b * 256 : (b + 1) * 256, :]).astype(BF)
            for r in range(8):
                rows_ref[b * count + 128 : (b + 1) * count, r * FOLD : (r + 1) * FOLD] = piece[r * 32 : (r + 1) * 32]
    for load in up_loads:
        load.wait()
    for c in range(units // part):
        cols = slice(c * part, (c + 1) * part)
        gate = dot(rows_ref[...], up_ref[:, cols])
        linear = dot(rows_ref[...], up_ref[:, units + c * part : units + (c + 1) * part])
        hidden_ref[:, cols] = (gate / (1.0 + jnp.exp(-gate)) * linear).astype(BF)
    down_load.wait()
    for c in range(width // FOLD):
        cols = slice(c * FOLD, (c + 1) * FOLD)
        made_ref[:, cols] = dot(hidden_ref[...], down_ref[:, cols]).astype(BF)
    copies = []
    fold_half = fold_half_matrix()
    for b in range(4):
        rows = slice(b * count, b * count + 128)
        for c in range(parts):
            cols = slice(c * FOLD, (c + 1) * FOLD)
            piece = jnp.concatenate(
                [made_ref[rows, cols], made_ref[rows, half + c * FOLD : half + (c + 1) * FOLD]], axis=0
            )
            sent_ref[b * 256 : (b + 1) * 256, cols] = dot(fold_half, piece).astype(BF)
        copies.append(block_copy(sent_ref, out_hbm, b, pl.ds(0, half), sems.at[b, 0]))
        copies[-1].start()
        if ninth:
            rows = slice(b * count + 128, (b + 1) * count)
            piece = jnp.concatenate([made_ref[rows, r * FOLD : (r + 1) * FOLD] for r in range(8)], axis=0)
            fold_ref[b * 256 : (b + 1) * 256, :] = dot(fold_matrix(), piece).astype(BF)
            copies.append(block_copy(fold_ref, out_hbm, b, pl.ds(half, FOLD), sems.at[b, 1]))
            copies[-1].start()
    for copy in copies:
        copy.wait()


def run_experts(arrived, up, down, part=256, chunks=4):
    width = up.shape[1]
    units = down.shape[1]
    half = width // 2
    ninth = arrived.shape[1] > half
    all_rows = 4 * (160 if ninth else 128)
    return pl.pallas_call(
        functools.partial(experts_kernel, ninth=ninth, part=part),
        in_specs=[pl.BlockSpec(memory_space=pl.ANY)] * 3,
        out_specs=pl.BlockSpec(memory_space=pl.ANY),
        out_shape=jax.ShapeDtypeStruct(arrived.shape, BF),
        scratch_shapes=[
            pltpu.VMEM((1024, half), BF),
            pltpu.VMEM((1024, FOLD), BF),
            pltpu.VMEM((all_rows, width), BF),
            pltpu.VMEM((width, 2 * units), BF),
            pltpu.VMEM((units, width), BF),
            pltpu.VMEM((all_rows, units), BF),
            pltpu.VMEM((all_rows, width), BF),
            pltpu.VMEM((1024, half), BF),
            pltpu.VMEM((1024, FOLD), BF),
            pltpu.SemaphoreType.DMA((4, 2)),
            pltpu.SemaphoreType.DMA((chunks,)),
            pltpu.SemaphoreType.DMA((1,)),
            pltpu.SemaphoreType.DMA((4, 2)),
        ],
        compiler_params=pltpu.CompilerParams(vmem_limit_bytes=VMEM),
        cost_estimate=pl.CostEstimate(
            flops=2 * all_rows * units * 3 * width, bytes_accessed=29_000_000, transcendentals=all_rows * units
        ),
        name="run_experts",
    )(arrived, up, down)


def first_combine_kernel(gates_ref, rows_ref, out_ref):
    tokens, width = out_ref.shape
    half = width // 2
    for c in range(half // FOLD):
        both = dot(gates_ref[...], rows_ref[:, c * FOLD : (c + 1) * FOLD])
        for h in range(2):
            at = h * half + c * FOLD
            out_ref[:, at : at + FOLD] = (
                both[h * tokens : (h + 1) * tokens] + both[(2 + h) * tokens : (3 + h) * tokens]
            )


def first_combine(gates, returned):
    tokens = gates.shape[0] // 4
    return pl.pallas_call(
        first_combine_kernel,
        out_shape=jax.ShapeDtypeStruct((tokens, 2 * returned.shape[1]), F32),
        compiler_params=pltpu.CompilerParams(vmem_limit_bytes=VMEM),
        cost_estimate=pl.CostEstimate(flops=2 * 512 * 1024 * 2048, bytes_accessed=7_500_000, transcendentals=0),
        name="first_combine",
    )(gates, returned)


def last_combine_kernel(
    gates_hbm, ninth_hbm, sum_hbm, rows_hbm, out_hbm,
    gates_ref, ninth_ref, sum_ref, rows_ref, last_ref, out_ref, row_sems, sems, out_sems,
):
    tokens, width = out_ref.shape
    half = width // 2
    parts = half // FOLD
    row_loads = []
    for b in range(4):
        rows = pl.ds(b * 256, 256)
        row_loads.append(pltpu.make_async_copy(rows_hbm.at[rows, :], rows_ref.at[rows, :], row_sems.at[b]))
        row_loads[-1].start()
    loads = [
        pltpu.make_async_copy(ninth_hbm, ninth_ref, sems.at[0]),
        pltpu.make_async_copy(gates_hbm, gates_ref, sems.at[1]),
        pltpu.make_async_copy(sum_hbm, sum_ref, sems.at[2]),
    ]
    for load in loads:
        load.start()
    unfold = unfold_matrix()
    for b in range(4):
        row_loads[b].wait()
        piece = dot(unfold, rows_ref[b * 256 : (b + 1) * 256, half:]).astype(BF)
        for r in range(8):
            last_ref[r, b * 32 : (b + 1) * 32, :] = piece[r * 32 : (r + 1) * 32]
    for load in loads:
        load.wait()
    copies = []
    for c in range(parts):
        both = dot(gates_ref[...], rows_ref[:, c * FOLD : (c + 1) * FOLD])
        for h in range(2):
            at = h * half + c * FOLD
            more = dot(ninth_ref[...], last_ref[h * parts + c])
            out_ref[:, at : at + FOLD] = (
                sum_ref[:, at : at + FOLD]
                + both[h * tokens : (h + 1) * tokens] + both[(2 + h) * tokens : (3 + h) * tokens]
                + more[:tokens] + more[tokens:]
            ).astype(BF)
            cols = pl.ds(at, FOLD)
            copies.append(pltpu.make_async_copy(out_ref.at[:, cols], out_hbm.at[:, cols], out_sems.at[c, h]))
            copies[-1].start()
    for copy in copies:
        copy.wait()


def last_combine(gates, ninth, total, returned):
    rows = returned.shape[0]
    tokens, width = total.shape
    return pl.pallas_call(
        last_combine_kernel,
        in_specs=[pl.BlockSpec(memory_space=pl.ANY)] * 4,
        out_specs=pl.BlockSpec(memory_space=pl.ANY),
        out_shape=jax.ShapeDtypeStruct((tokens, width), BF),
        scratch_shapes=[
            pltpu.VMEM(gates.shape, BF),
            pltpu.VMEM(ninth.shape, BF),
            pltpu.VMEM(total.shape, F32),
            pltpu.VMEM(returned.shape, BF),
            pltpu.VMEM((8, 128, FOLD), BF),
            pltpu.VMEM((tokens, width), BF),
            pltpu.SemaphoreType.DMA((rows // 256,)),
            pltpu.SemaphoreType.DMA((3,)),
            pltpu.SemaphoreType.DMA((width // 2 // FOLD, 2)),
        ],
        compiler_params=pltpu.CompilerParams(vmem_limit_bytes=VMEM),
        cost_estimate=pl.CostEstimate(flops=2 * 512 * 1152 * 2048, bytes_accessed=10_000_000, transcendentals=0),
        name="last_combine",
    )(gates, ninth, total, returned)


def attention_kernel(place_ref, queries_ref, keys_ref, values_ref, out_ref):
    rows = queries_ref.shape[0]
    heads = queries_ref.shape[1] // HEAD_SIZE
    ahead = iota((rows, rows), 1) - iota((rows, rows), 0)
    seen = jnp.concatenate(
        [ahead <= (place_ref[0] - place_ref[j]) * rows for j in range(keys_ref.shape[0] // rows)], axis=1
    )
    factor = HEAD_SIZE**-0.5 * 1.4426950408889634
    for h in range(heads):
        cols = slice(h * HEAD_SIZE, (h + 1) * HEAD_SIZE)
        scores = lax.dot_general(
            queries_ref[:, cols], keys_ref[...], (((1,), (1,)), ((), ())), preferred_element_type=F32
        )
        scores = jnp.where(seen, scores, -1e30)
        top = jnp.max(scores, axis=-1, keepdims=True)
        part = jnp.exp2((scores - top) * factor)
        total = jnp.sum(part, axis=-1, keepdims=True)
        mixed = dot(part.astype(BF), values_ref[...])
        out_ref[:, cols] = (mixed / total).astype(BF)


def attention(places, queries, pairs, heads_per_step=16):
    rows, width = queries.shape
    length = pairs.shape[0]
    kv_heads = pairs.shape[1] // (2 * HEAD_SIZE)
    steps = width // (heads_per_step * HEAD_SIZE)
    per_kv = steps // kv_heads
    block = (rows, heads_per_step * HEAD_SIZE)
    return pl.pallas_call(
        attention_kernel,
        grid=(steps,),
        in_specs=[
            pl.BlockSpec(memory_space=pltpu.SMEM),
            pl.BlockSpec(block, lambda i: (0, i)),
            pl.BlockSpec((length, HEAD_SIZE), lambda i: (0, i // per_kv)),
            pl.BlockSpec((length, HEAD_SIZE), lambda i: (0, kv_heads + i // per_kv)),
        ],
        out_specs=pl.BlockSpec(block, lambda i: (0, i)),
        out_shape=jax.ShapeDtypeStruct(queries.shape, BF),
        compiler_params=pltpu.CompilerParams(vmem_limit_bytes=VMEM),
        cost_estimate=pl.CostEstimate(
            flops=4 * rows * width * length, bytes_accessed=9_000_000, transcendentals=rows * length * width // HEAD_SIZE
        ),
        name="attention_rows",
    )(places, queries, pairs, pairs)


def at(y, z, core):
    return y * 8 + (z % 4) * 2 + core


def moved(rows, dy=0, dz=0, dcore=0):
    pairs = [
        (at(y, z, core), at((y + dy) % 2, z + dz, (core + dcore) % 2))
        for y in range(2) for z in range(4) for core in range(2)
    ]
    return lax.ppermute(rows, "seq", pairs)


def exchange(rows):
    return lax.all_to_all(rows, ("seq", "exp"), split_axis=0, concat_axis=0, tiled=True)


def on_device(queries, keys, values, tokens, routed, gates, up, down):
    tied = lax.optimization_barrier
    block = keys.shape[1]
    routed, gates = routed.T, gates.T
    pairs = jnp.concatenate([keys[0], values[0]], axis=1)
    across = moved(pairs, dy=1)
    outgoing = dispatch(routed, tokens, False)

    outgoing, pairs, across, routed, tokens = tied((outgoing, pairs, across, routed, tokens))
    arrived_1 = exchange(outgoing)
    outgoing = dispatch(routed, tokens, True)
    here = jnp.concatenate([pairs, across], axis=0)
    below, above = moved(here, dz=1), moved(here, dz=-1)

    arrived_1, outgoing, here, below, above = tied((arrived_1, outgoing, here, below, above))
    arrived_2 = exchange(outgoing)
    made = run_experts(arrived_1, up, down)
    far = [moved(below[:block], dz=1), moved(above[block:], dz=-1)]

    arrived_2, made, here, below, above, far = tied((arrived_2, made, here, below, above, far))
    returned_1 = exchange(made)
    made = run_experts(arrived_2, up, down)
    column = jnp.concatenate([here, below, above, *far], axis=0)
    other = moved(column, dcore=1)

    returned_1, made, column, other, routed, gates, own = tied(
        (returned_1, made, column, other, routed, gates, queries[0])
    )
    returned_2 = exchange(made)
    weights_1, weights_2, weights_3 = gate_matrices(routed, gates)
    total = first_combine(weights_1, returned_1)
    index = lax.axis_index("seq")
    y, z, core = index // 8, index // 2 % 4, index % 2
    places = [
        at((y + dy) % 2, z + dz, (core + dcore) % 2) for dcore in range(2) for dz in (0, -1, 1, 2) for dy in range(2)
    ]
    whole = jnp.concatenate([column, other], axis=0)
    attended = attention(jnp.stack(places).astype(jnp.int32), own, whole)
    return (attended[None], last_combine(weights_2, weights_3, total, returned_2))


def solution(mesh):
    spread = P(("seq", "exp"), None)
    in_specs = (P("exp", "seq", None),) * 3 + (spread,) * 3 + (P(("seq", "exp"), None, None),) * 2
    out_specs = (P("exp", "seq", None), spread)
    return jax.shard_map(on_device, mesh=mesh, in_specs=in_specs, out_specs=out_specs, check_vma=False)
```

time: 355 us -> 301 us (0.85)
  the two profiles are of different devices: /device:TPU:39 before, /device:TPU:6 now
where the time goes in v3:
time: 301 us; the launch traced here: 295 us
  waiting for transfers between devices  142 us (47%)
  Pallas kernels  101 us (34%)
  starting transfers between devices  43 us (14%)
  other arithmetic  5.07 us (2%)
    ppermute x6, waiting for transfers between devices, moved(): return lax.ppermute(rows, 'seq', pairs)  95.6 us
    all_to_all x4, waiting for transfers between devices, exchange(): lax.all_to_all(rows, ('seq', 'exp'), split_axis=0, concat_axis=0, tiled=T...  46 us
    pallas_call x2, Pallas kernels, run_experts(): pl.pallas_call(functools.partial(experts_kernel, ninth=ninth, part=part),...  39.9 us
    pallas_call x1, Pallas kernels, attention(): pl.pallas_call(attention_kernel, grid=(steps,), in_specs=[pl.BlockSpec(me...  35.4 us
    all_to_all x4, starting transfers between devices, exchange(): lax.all_to_all(rows, ('seq', 'exp'), split_axis=0, concat_axis=0, tiled=T...  33.6 us
    pallas_call x2, Pallas kernels, dispatch(): pl.pallas_call(functools.partial(dispatch_kernel, first=HALF * second, ni...  9.84 us
    ppermute x6, starting transfers between devices, moved(): return lax.ppermute(rows, 'seq', pairs)  9.34 us
    pallas_call x1, Pallas kernels, last_combine(): pl.pallas_call(last_combine_kernel, in_specs=[pl.BlockSpec(memory_space=p...  7.15 us
  transfers between devices with their start and end apart: 10, of which 6 were waited for; matrix products, arithmetic and copies ran while one was open for 2% of the time, Pallas kernels for 32%

profile of v3, /device:TPU:6, one launch (start us, length us, event | category | flops | bytes accessed | tf_op | source)
XLA Modules:
  0.0 295.3 jit_solution(10673237032008548537)
XLA Ops:
  0.6 1.0 pad_maximum_fusion.1
  1.6 1.7 collective-permute-start
  3.3 4.7 %dispatch_rows.2 = bf16[1024,2048]{1,0:T(8,128)(2,1)} custom-call(s32[8,128]{1,0:T(8,128)} %bitcast.36, bf16[128,4096]{1,0:T(8,128)(2,1)} %tokens_hbm.2), custom_call_target="tpu_custom_call" | custom-call | flops 671088640 | bytes 6000000 | tf_op jit(solution)/shard_map/dispatch_rows/pallas_call | solution.py:112
  8.0 1.8 collective-permute-done
  9.8 10.9 %all-to-all-start = ((bf16[128,8,2048]{2,1,0:T(8,128)(2,1)}), bf16[128,8,2048]{2,1,0:T(8,128)(2,1)}, u32[]{:S(2)}, u32[]{:S(2)}) async-start(bf16[128,8,2048]{2,1,0:T(8,128)(2,1)} %bitcast.31), calls=%async_computation | async-start | bytes 8388608 | tf_op jit(solution)/shard_map/all_to_all | solution.py:441
  20.7 0.0 copy-start
  20.8 1.7 collective-permute-start.1
  22.5 1.8 collective-permute-start.2
  24.3 5.1 %dispatch_rows.3 = bf16[1024,2560]{1,0:T(8,128)(2,1)} custom-call(s32[8,128]{1,0:T(8,128)} %bitcast.37, bf16[128,4096]{1,0:T(8,128)(2,1)} %tokens_hbm.2), custom_call_target="tpu_custom_call" | custom-call | flops 671088640 | bytes 6000000 | tf_op jit(solution)/shard_map/dispatch_rows/pallas_call | solution.py:112
  29.4 0.0 copy-done
  29.4 51.1 %collective-permute-done.1 = bf16[256,1024]{1,0:T(8,128)(2,1)S(1)} collective-permute-done((bf16[256,1024]{1,0:T(8,128)(2,1)S(1)}, bf16[256,1024]{1,0:T(8,128)(2,1)S(1)}, u32[]{:S(2)}, u32[]{:S(2)}) %collective-permute-start.1) | collective-permute-done | bytes 524320 | tf_op jit(solution)/shard_map/ppermute | solution.py:437
  80.6 0.0 collective-permute-done.2
  80.6 0.0 all-to-all-done
  80.6 7.9 %all-to-all-start.1 = ((bf16[128,8,2560]{2,1,0:T(8,128)(2,1)}), bf16[128,8,2560]{2,1,0:T(8,128)(2,1)}, u32[]{:S(2)}, u32[]{:S(2)}) async-start(bf16[128,8,2560]{2,1,0:T(8,128)(2,1)} %bitcast.30), calls=%async_computation.1 | async-start | bytes 10485760 | tf_op jit(solution)/shard_map/all_to_all | solution.py:441
  88.5 1.7 collective-permute-start.3
  90.2 2.0 collective-permute-start.4
  92.2 18.4 %run_experts.2 = bf16[1024,2048]{1,0:T(8,128)(2,1)} custom-call(bf16[1024,2048]{1,0:T(8,128)(2,1)} %bitcast.20.rows_hbm, bf16[1,4096,1536]{2,1,0:T(8,128)(2,1)} %up_hbm.3, bf16[1,768,4096]{2,1,0:T(8,128)(2,1)} %down_hbm.3), custom_call_target="tpu_custom_call" | custom-call | flops 9663676416 | bytes 29000000 | tf_op jit(solution)/shard_map/run_experts/pallas_call | solution.py:260
  110.6 42.7 %collective-permute-done.3 = bf16[128,1024]{1,0:T(8,128)(2,1)S(1)} collective-permute-done((bf16[128,1024]{1,0:T(8,128)(2,1)S(1)}, bf16[128,1024]{1,0:T(8,128)(2,1)S(1)}, u32[]{:S(2)}, u32[]{:S(2)}) %collective-permute-start.3) | collective-permute-done | bytes 262176 | tf_op jit(solution)/shard_map/ppermute | solution.py:437
  153.3 0.0 collective-permute-done.4
  153.3 2.6 all-to-all-done.1
  155.9 7.2 %all-to-all-start.2 = ((bf16[128,8,2048]{2,1,0:T(8,128)(2,1)}), bf16[128,8,2048]{2,1,0:T(8,128)(2,1)}, u32[]{:S(2)}, u32[]{:S(2)}) async-start(bf16[128,8,2048]{2,1,0:T(8,128)(2,1)} %bitcast.33), calls=%async_computation.2 | async-start | bytes 8388608 | tf_op jit(solution)/shard_map/all_to_all | solution.py:441
  163.1 1.1 constant_dynamic-update-slice_fusion.6
  164.3 1.0 constant_dynamic-update-slice_fusion.2
  165.3 0.4 collective-permute-start.5
  165.7 21.5 %run_experts.3 = bf16[1024,2560]{1,0:T(8,128)(2,1)} custom-call(bf16[1024,2560]{1,0:T(8,128)(2,1)} %bitcast.22.rows_hbm, bf16[1,4096,1536]{2,1,0:T(8,128)(2,1)} %up_hbm.3, bf16[1,768,4096]{2,1,0:T(8,128)(2,1)} %down_hbm.3), custom_call_target="tpu_custom_call" | custom-call | flops 12079595520 | bytes 29000000 | tf_op jit(solution)/shard_map/run_experts/pallas_call | solution.py:260
  187.3 0.0 collective-permute-done.5
  187.3 27.4 %all-to-all-done.2 = bf16[128,8,2048]{2,1,0:T(8,128)(2,1)} async-done(((bf16[128,8,2048]{2,1,0:T(8,128)(2,1)}), bf16[128,8,2048]{2,1,0:T(8,128)(2,1)}, u32[]{:S(2)}, u32[]{:S(2)}) %all-to-all-start.2) | async-done | bytes 4194336 | tf_op jit(solution)/shard_map/all_to_all | solution.py:441
  214.7 7.6 %all-to-all-start.3 = ((bf16[128,8,2560]{2,1,0:T(8,128)(2,1)}), bf16[128,8,2560]{2,1,0:T(8,128)(2,1)}, u32[]{:S(2)}, u32[]{:S(2)}) async-start(bf16[128,8,2560]{2,1,0:T(8,128)(2,1)} %bitcast.32), calls=%async_computation.3 | async-start | bytes 10485760 | tf_op jit(solution)/shard_map/all_to_all | solution.py:441
  222.4 0.7 stack.67.place_ref
  223.1 2.9 gate_matrices.1
  226.0 6.1 %first_combine.1.sum_hbm = f32[128,4096]{1,0:T(8,128)} custom-call(bf16[512,1024]{1,0:T(8,128)(2,1)} %get-tuple-element.53.gates_ref, bf16[1024,2048]{1,0:T(8,128)(2,1)} %bitcast.24.rows_ref), custom_call_target="tpu_custom_call" | custom-call | flops 2147483648 | bytes 7500000 | tf_op jit(solution)/shard_map/first_combine/pallas_call | solution.py:302
  232.1 4.1 %pad_maximum_fusion.keys_ref.values_ref = bf16[2048,1024]{1,0:T(8,128)(2,1)} fusion(bf16[1024,1024]{1,0:T(8,128)(2,1)} %collective-permute-done.5, bf16[1024,1024]{1,0:T(8,128)(2,1)S(1)} %constant_dynamic-update-slice_fusion.2), kind=kLoop, calls=%fused_computation | loop fusion | flops 8388608 | bytes 8388608 | tf_op jit(solution)/shard_map/concatenate | solution.py:480
  236.2 35.4 %attention_rows.1 = bf16[128,8192]{1,0:T(8,128)(2,1)} custom-call(s32[16]{0:T(128)} %stack.67.place_ref, bf16[128,8192]{1,0:T(8,128)(2,1)} %bitcast.39, bf16[2048,1024]{1,0:T(8,128)(2,1)} %pad_maximum_fusion.keys_ref.values_ref, bf16[2048,1024]{1,0:T(8,128)(2,1)} %pad_maximum_fusion.keys_ref.values_ref), custom_call_target="tpu_custom_call" | custom-call | flops 8589934592 | bytes 9000000 | tf_op jit(solution)/shard_map/attention_rows/pallas_call | solution.py:409
  271.6 16.1 %all-to-all-done.3 = bf16[128,8,2560]{2,1,0:T(8,128)(2,1)} async-done(((bf16[128,8,2560]{2,1,0:T(8,128)(2,1)}), bf16[128,8,2560]{2,1,0:T(8,128)(2,1)}, u32[]{:S(2)}, u32[]{:S(2)}) %all-to-all-start.3) | async-done | bytes 5242912 | tf_op jit(solution)/shard_map/all_to_all | solution.py:441
  287.7 7.2 %last_combine.1 = bf16[128,4096]{1,0:T(8,128)(2,1)} custom-call(bf16[512,1024]{1,0:T(8,128)(2,1)} %get-tuple-element.51.gates_hbm, bf16[256,128]{1,0:T(8,128)(2,1)} %get-tuple-element.52.ninth_hbm, f32[128,4096]{1,0:T(8,128)} %first_combine.1.sum_hbm, bf16[1024,2560]{1,0:T(8,128)(2,1)} %bitcast.29.rows_hbm), custom_call_target="tpu_custom_call" | custom-call | flops 2415919104 | bytes 10000000 | tf_op jit(solution)/shard_map/last_combine/pallas_call | solution.py:359
  (7 shorter events, 0.2 us)
Async XLA Ops:
  1.6 8.1 %collective-permute-start = (bf16[128,1024]{1,0:T(8,128)(2,1)S(1)}, bf16[128,1024]{1,0:T(8,128)(2,1)S(1)}, u32[]{:S(2)}, u32[]{:S(2)}) collective-permute-start(bf16[128,1024]{1,0:T(8,128)(2,1)S(1)} %pad_maximum_fusion.1), channel_id=1, source_target_pairs={{0,64},{8,72},{16,80},{24,88},{32,96},{40,104},{48,112},{56,120},{... | collective-permute-start | bytes 786440 | tf_op jit(solution)/shard_map/ppermute | solution.py:437
  9.8 70.8 %all-to-all-start = ((bf16[128,8,2048]{2,1,0:T(8,128)(2,1)}), bf16[128,8,2048]{2,1,0:T(8,128)(2,1)}, u32[]{:S(2)}, u32[]{:S(2)}) async-start(bf16[128,8,2048]{2,1,0:T(8,128)(2,1)} %bitcast.31), calls=%async_computation | async-start | bytes 8388608 | tf_op jit(solution)/shard_map/all_to_all | solution.py:441
  20.7 8.7 %copy-start = (bf16[256,1024]{1,0:T(8,128)(2,1)}, bf16[256,1024]{1,0:T(8,128)(2,1)S(1)}, u32[]{:S(2)}) copy-start(bf16[256,1024]{1,0:T(8,128)(2,1)S(1)} %constant_dynamic-update-slice_fusion) | copy-start | bytes 1572868
  20.8 59.8 %collective-permute-start.1 = (bf16[256,1024]{1,0:T(8,128)(2,1)S(1)}, bf16[256,1024]{1,0:T(8,128)(2,1)S(1)}, u32[]{:S(2)}, u32[]{:S(2)}) collective-permute-start(bf16[256,1024]{1,0:T(8,128)(2,1)S(1)} %constant_dynamic-update-slice_fusion), channel_id=1, source_target_pairs={{0,16},{8,24},{16,32},{24,40},{32,48},{40,56},{48,0},{56,8},{64,80... | collective-permute-start | bytes 1572872 | tf_op jit(solution)/shard_map/ppermute | solution.py:437
  22.5 58.1 %collective-permute-start.2 = (bf16[256,1024]{1,0:T(8,128)(2,1)S(1)}, bf16[256,1024]{1,0:T(8,128)(2,1)S(1)}, u32[]{:S(2)}, u32[]{:S(2)}) collective-permute-start(bf16[256,1024]{1,0:T(8,128)(2,1)S(1)} %constant_dynamic-update-slice_fusion), channel_id=1, source_target_pairs={{0,48},{8,56},{16,0},{24,8},{32,16},{40,24},{48,32},{56,40},{64,11... | collective-permute-start | bytes 1572872 | tf_op jit(solution)/shard_map/ppermute | solution.py:437
  80.6 75.3 %all-to-all-start.1 = ((bf16[128,8,2560]{2,1,0:T(8,128)(2,1)}), bf16[128,8,2560]{2,1,0:T(8,128)(2,1)}, u32[]{:S(2)}, u32[]{:S(2)}) async-start(bf16[128,8,2560]{2,1,0:T(8,128)(2,1)} %bitcast.30), calls=%async_computation.1 | async-start | bytes 10485760 | tf_op jit(solution)/shard_map/all_to_all | solution.py:441
  88.5 64.8 %collective-permute-start.3 = (bf16[128,1024]{1,0:T(8,128)(2,1)S(1)}, bf16[128,1024]{1,0:T(8,128)(2,1)S(1)}, u32[]{:S(2)}, u32[]{:S(2)}) collective-permute-start(bf16[128,1024]{1,0:T(8,128)(2,1)S(1)} %slice.6), channel_id=1, source_target_pairs={{0,16},{8,24},{16,32},{24,40},{32,48},{40,56},{48,0},{56,8},{64,80... | collective-permute-start | bytes 786440 | tf_op jit(solution)/shard_map/ppermute | solution.py:437
  90.2 63.1 %collective-permute-start.4 = (bf16[128,1024]{1,0:T(8,128)(2,1)S(1)}, bf16[128,1024]{1,0:T(8,128)(2,1)}, u32[]{:S(2)}, u32[]{:S(2)}) collective-permute-start(bf16[128,1024]{1,0:T(8,128)(2,1)S(1)} %slice.7), channel_id=1, source_target_pairs={{0,48},{8,56},{16,0},{24,8},{32,16},{40,24},{48,32},{56,40},{64,11... | collective-permute-start | bytes 786440 | tf_op jit(solution)/shard_map/ppermute | solution.py:437
  155.9 58.7 %all-to-all-start.2 = ((bf16[128,8,2048]{2,1,0:T(8,128)(2,1)}), bf16[128,8,2048]{2,1,0:T(8,128)(2,1)}, u32[]{:S(2)}, u32[]{:S(2)}) async-start(bf16[128,8,2048]{2,1,0:T(8,128)(2,1)} %bitcast.33), calls=%async_computation.2 | async-start | bytes 8388608 | tf_op jit(solution)/shard_map/all_to_all | solution.py:441
  165.3 22.0 %collective-permute-start.5 = (bf16[1024,1024]{1,0:T(8,128)(2,1)S(1)}, bf16[1024,1024]{1,0:T(8,128)(2,1)}, u32[]{:S(2)}, u32[]{:S(2)}) collective-permute-start(bf16[1024,1024]{1,0:T(8,128)(2,1)S(1)} %constant_dynamic-update-slice_fusion.2), channel_id=1, source_target_pairs={{0,8},{8,0},{16,24},{24,16},{32,40},{40,32},{48,56},{56,48},{64,72... | collective-permute-start | bytes 6291464 | tf_op jit(solution)/shard_map/ppermute | solution.py:437
  214.7 73.0 %all-to-all-start.3 = ((bf16[128,8,2560]{2,1,0:T(8,128)(2,1)}), bf16[128,8,2560]{2,1,0:T(8,128)(2,1)}, u32[]{:S(2)}, u32[]{:S(2)}) async-start(bf16[128,8,2560]{2,1,0:T(8,128)(2,1)} %bitcast.32), calls=%async_computation.3 | async-start | bytes 10485760 | tf_op jit(solution)/shard_map/all_to_all | solution.py:441
